TPU v7x, 32 devices: a whole 2x2x4 slice. The times are simulated.
32 devices in a mesh: rep: 2 (over x), store: 8 (over z, y), tensor: 2 (over core).
Axes of the slice: x: 2, y: 2, z: 4, core: 2. Of those that a mesh axis runs over, the one named last changes fastest.
Arguments:
- queries: bfloat16 [384, 4, 32, 128], P(('rep', 'store'), None, 'tensor'), parts along dimension 0, may hold values from -24 to 24
- kv_cache: bfloat16 [2, 384, 4, 256, 128], P(None, ('rep', 'store'), 'tensor'), parts along dimension 1, may hold values from -12 to 12
- new_kv: bfloat16 [2, 384, 4, 4, 128], P(None, ('rep', 'store'), None, 'tensor'), parts along dimension 1, may hold values from -12 to 12
- lengths: int32 [384], P(('rep', 'store')), parts along dimension 0, may hold values from 1 to 256, 24576 in all
- adapter_ids: int32 [384], P(('rep', 'store')), parts along dimension 0, may hold values from 0 to 63, as said below
- place: int32 [128], P('rep'), parts along dimension 0, may hold values from 0 to 63, as said below
- ranks: int32 [128], P('rep'), parts along dimension 0, may hold values from 4 to 64
- w_out: bfloat16 [4096, 4096], P('tensor'), may hold values from -0.09375 to 0.09375
- a_store: bfloat16 [128, 4096, 64], P(('rep', 'store'), 'tensor'), parts along dimension 0, may hold values from -0.09375 to 0.09375
- b_store: bfloat16 [128, 64, 4096], P(('rep', 'store'), None, 'tensor'), parts along dimension 0, may hold values from -0.75 to 0.75
Outputs:
- mixed: bfloat16 [384, 4, 4096], P(('rep', 'store'), None, 'tensor'), parts along dimension 0
There are 2 independent parts, one for each index of `rep`. A program takes and returns all parts, laid end to end along the dimension named above; an argument that names none is the same for every part. Nothing has to cross between parts.
Inputs may be any that keep to these rules, and one draw needn't show every extreme that they name: Adapter a's factor blocks stand at position place[a] of a_store and b_store; each position once. `adapter_ids`: among the 24 requests of one group, at most 3 use adapters placed with one owner (place // 8), and those name at most 2 distinct adapters; both bounds are reached in every group.
All inputs are finite; a program needn't handle non-finite values. No bound on the sum of `lengths` on one device may be relied on, other than what follows from the above.
Results may differ from a plain program's by a relative error of at most 0.008.
Values may be sent and summed in bfloat16 or wider, within the bound.
No kernel may reach another device: no remote copies, remote signals or barrier semaphores. Data moves between devices by JAX's collectives and lax.ppermute only.
A program may use at most 128 MiB of HBM per device.

v0:
```python
import math

import jax
import jax.numpy as jnp
from jax import lax
from jax.sharding import PartitionSpec as P

ACAP = 2


adapter_scale = 8.0


def rank_factor(request_rank, width):
    column_indices = jnp.arange(width, dtype=jnp.int32)
    rank_as_real = request_rank.astype(jnp.float32)[..., None]
    return jnp.where(
        column_indices < request_rank[..., None], adapter_scale / jnp.sqrt(rank_as_real), 0.0
    )


def lookup(table, index):
    hits = index[:, None] == jnp.arange(table.shape[0], dtype=jnp.int32)[None, :]
    return jnp.sum(jnp.where(hits, table[None, :], 0), axis=1)


def attend(queries, kv_cache, new_kv, lengths):
    request_count, step_count, head_count, head_size = queries.shape
    key_heads = kv_cache.shape[2]
    cache_slots = kv_cache.shape[3]
    grouped = queries.reshape(
        request_count, step_count, key_heads, head_count // key_heads, head_size
    )
    score_scale = 1.0 / math.sqrt(head_size)
    cached = (
        jnp.einsum("rsngd,rncd->rsngc", grouped, kv_cache[0], preferred_element_type=jnp.float32)
        * score_scale
    )
    visible = jnp.arange(cache_slots, dtype=jnp.int32)[None, :] < lengths[:, None]
    cached = jnp.where(visible[:, None, None, None, :], cached, -jnp.inf)
    new_scores = (
        jnp.einsum("rsngd,rtnd->rsngt", grouped, new_kv[0], preferred_element_type=jnp.float32)
        * score_scale
    )
    causal = jnp.arange(step_count)[:, None] >= jnp.arange(step_count)[None, :]
    new_scores = jnp.where(causal[None, :, None, None, :], new_scores, -jnp.inf)
    scores = jnp.concatenate([cached, new_scores], axis=-1)
    row_max = jnp.max(scores, axis=-1, keepdims=True)
    exponent = jnp.exp(scores - row_max)
    weights_bf = (exponent / jnp.sum(exponent, axis=-1, keepdims=True)).astype(jnp.bfloat16)
    attended = jnp.einsum(
        "rsngc,rncd->rsngd",
        weights_bf[..., :cache_slots],
        kv_cache[1],
        preferred_element_type=jnp.float32,
    )
    attended = attended + jnp.einsum(
        "rsngt,rtnd->rsngd",
        weights_bf[..., cache_slots:],
        new_kv[1],
        preferred_element_type=jnp.float32,
    )
    return attended.reshape(request_count, step_count, head_count * head_size).astype(jnp.bfloat16)


def local(queries, kv_cache, new_kv, lengths, adapter_ids, place, ranks, w_out, a_store, b_store):
    request_count, step_count = (queries.shape[0], queries.shape[1])
    attended = attend(queries, kv_cache, new_kv, lengths)
    feature_half = attended.shape[2]
    out_half = b_store.shape[2]
    rank_width = a_store.shape[2]
    partial_out = jnp.dot(
        attended.reshape(request_count * step_count, feature_half),
        w_out,
        preferred_element_type=jnp.float32,
    )
    plain_projection_sum = lax.psum_scatter(
        partial_out, "tensor", scatter_dimension=1, tiled=True
    ).reshape(request_count, step_count, out_half)
    owners = lax.axis_size("store")
    per_owner = a_store.shape[0]
    location = lookup(place, adapter_ids)
    request_rank = lookup(ranks, adapter_ids)
    owner_of = location // per_owner
    slot_of = location % per_owner
    order_index = jnp.arange(request_count, dtype=jnp.int32)
    earlier = order_index[None, :] < order_index[:, None]
    same_owner = owner_of[:, None] == owner_of[None, :]
    owner_range = jnp.arange(owners, dtype=jnp.int32)
    same_loc = location[:, None] == location[None, :]
    leading = jnp.logical_not(jnp.any(same_loc & earlier, axis=1))
    lead_rank = jnp.sum(same_owner & earlier & leading[None, :], axis=1)
    fetch_col = jnp.sum(jnp.where(same_loc & leading[None, :], lead_rank[None, :], 0), axis=1)
    hits = leading[:, None, None] & (owner_of[:, None, None] == owner_range[None, :, None])
    hits = hits & (lead_rank[:, None, None] == jnp.arange(ACAP, dtype=jnp.int32)[None, None, :])
    wanted = jnp.sum(jnp.where(hits, slot_of[:, None, None], 0), axis=0)
    asked = lax.all_to_all(wanted, "store", split_axis=0, concat_axis=0, tiled=True)
    got_first, got_second = (
        lax.all_to_all(a_store[asked], "store", split_axis=0, concat_axis=0, tiled=True),
        lax.all_to_all(b_store[asked], "store", split_axis=0, concat_axis=0, tiled=True),
    )
    flat_index = owner_of * ACAP + fetch_col
    first_req = got_first.reshape(owners * ACAP, feature_half, rank_width)[flat_index]
    second_request = got_second.reshape(owners * ACAP, rank_width, out_half)[flat_index]
    partial_value = jnp.einsum(
        "rsh,rhk->rsk", attended, first_req, preferred_element_type=jnp.float32
    )
    summed = lax.psum(partial_value, "tensor")
    narrow_product = (summed * rank_factor(request_rank, rank_width)[:, None, :]).astype(
        jnp.bfloat16
    )
    adapter_update = jnp.einsum(
        "hpx,hxg->hpg", narrow_product, second_request, preferred_element_type=jnp.float32
    ).astype(jnp.bfloat16)
    adapter_update = adapter_update.astype(jnp.float32)
    return (plain_projection_sum + adapter_update).astype(jnp.bfloat16)


def solution(mesh):
    return jax.shard_map(
        local,
        mesh=mesh,
        in_specs=(
            P(("rep", "store"), None, "tensor", None),
            P(None, ("rep", "store"), "tensor", None, None),
            P(None, ("rep", "store"), None, "tensor", None),
            P(("rep", "store")),
            P(("rep", "store")),
            P("rep"),
            P("rep"),
            P("tensor", None),
            P(("rep", "store"), "tensor", None),
            P(("rep", "store"), None, "tensor"),
        ),
        out_specs=P(("rep", "store"), None, "tensor"),
        check_vma=False,
    )
```

profile of v0, /device:TPU:0, one launch (start us, length us, event | category | flops | bytes accessed | tf_op | source)
XLA Modules:
  0.0 236.8 jit_solution(10674276157656768748)
XLA Ops:
  6.5 1.0 select_reduce_fusion
  8.2 13.5 %all_to_all.22 = s32[8,1,2]{2,1,0:T(1,128)S(1)} all-to-all(s32[8,1,2]{2,1,0:T(1,128)S(1)} %copy.88), channel_id=1, replica_groups=mesh['rep'=2,'store'=8,'tensor'=2] {'store'}, dimensions={0} | all-to-all | bytes 128 | tf_op jit(solution)/shard_map/all_to_all | solution.py:97
  22.0 2.7 %gather_fusion = bf16[16,2048,64]{1,2,0:T(8,128)(2,1)} fusion(bf16[8,2048,64]{1,2,0:T(8,128)(2,1)S(1)} %copy-done, s32[1024]{0:T(1024)S(1)} %pad_clamp_fusion.1), kind=kCustom, calls=%fused_computation | custom fusion | bytes 8388672 | tf_op jit(solution)/shard_map/gather | solution.py:99
  24.8 4.7 %all-to-all-start.1 = ((bf16[8,2,2048,64]{2,3,1,0:T(8,128)(2,1)}), bf16[8,2,2048,64]{2,3,1,0:T(8,128)(2,1)}, u32[]{:S(2)}, u32[]{:S(2)}) async-start(bf16[8,2,2048,64]{2,3,1,0:T(8,128)(2,1)} %bitcast.82), calls=%async_computation.2 | async-start | bytes 8388608 | tf_op jit(solution)/shard_map/all_to_all | solution.py:99
  29.5 2.9 %gather_fusion.2 = bf16[16,64,2048]{2,1,0:T(8,128)(2,1)} fusion(bf16[8,64,2048]{2,1,0:T(8,128)(2,1)S(1)} %copy-done.2, s32[1024]{0:T(1024)S(1)} %pad_clamp_fusion.1), kind=kCustom, calls=%fused_computation.2 | custom fusion | bytes 8388672 | tf_op jit(solution)/shard_map/gather | solution.py:100
  32.4 89.1 %all-to-all-done.1 = bf16[8,2,2048,64]{2,3,1,0:T(8,128)(2,1)} async-done(((bf16[8,2,2048,64]{2,3,1,0:T(8,128)(2,1)}), bf16[8,2,2048,64]{2,3,1,0:T(8,128)(2,1)}, u32[]{:S(2)}, u32[]{:S(2)}) %all-to-all-start.1) | async-done | bytes 4194336 | tf_op jit(solution)/shard_map/all_to_all | solution.py:99
  121.5 4.7 %all-to-all-start.2 = ((bf16[8,2,64,2048]{3,2,1,0:T(8,128)(2,1)}), bf16[8,2,64,2048]{3,2,1,0:T(8,128)(2,1)}, u32[]{:S(2)}, u32[]{:S(2)}) async-start(bf16[8,2,64,2048]{3,2,1,0:T(8,128)(2,1)} %bitcast.83), calls=%async_computation.3 | async-start | bytes 8388608 | tf_op jit(solution)/shard_map/all_to_all | solution.py:100
  126.3 1.8 fusion.25
  128.2 0.3 copy.81
  128.7 0.8 copy.82
  129.6 3.1 %fusion.37 = (f32[24,4,2,8]{3,1,2,0:T(4,128)S(1)}, f32[24,4,2,8,256]{4,3,1,2,0:T(8,128)S(1)}) fusion(bf16[2,24,2,256,128]{4,3,2,1,0:T(8,128)(2,1)} %param.11, pred[24,256]{1,0:T(8,128)(4,1)S(1)} %iota_compare_fusion, bf16[24,4,16,128]{3,2,1,0:T(8,128)(2,1)S(1)} %copy-done.3), kind=kOutput, calls=%fused_computation.71 | convolution fusion | flops 101841408 | bytes 5124096 | tf_op jit(solution)/shard_map/rsngd,rncd->rsngc/dot_general | solution.py:36
  132.8 0.9 fusion.10
  133.7 0.6 divide_convert_fusion
  134.3 0.2 fusion.23
  134.6 2.4 %fusion.19 = bf16[24,4,2,8,128]{4,3,1,2,0:T(8,128)(2,1)S(1)} fusion(f32[24,2,4,8,128]{4,3,2,1,0:T(8,128)S(1)} %fusion.23, bf16[2,24,2,256,128]{4,3,2,1,0:T(8,128)(2,1)} %param.11, bf16[24,4,2,8,260]{4,3,1,2,0:T(8,128)(2,1)S(1)} %divide_convert_fusion), kind=kOutput, calls=%fused_computation.21 | convolution fusion | flops 101056512 | bytes 5111808 | tf_op jit(solution)/shard_map/rsngc,rncd->rsngd/dot_general | solution.py:51
  137.3 9.7 %fusion.38 = f32[96,4096]{1,0:T(8,128)} fusion(bf16[96,2048]{1,0:T(8,128)(2,1)S(1)} %convert_element_type.42, bf16[2048,4096]{1,0:T(8,128)(2,1)} %param.17), kind=kOutput, calls=%fused_computation.72 | convolution fusion | flops 1610612736 | bytes 18743296 | tf_op jit(solution)/shard_map/dot_general | solution.py:72
  147.4 10.1 %reduce-scatter.2.cloned.1.call-done = f32[96,2048]{1,0:T(8,128)} async-done(((f32[96,4096]{1,0:T(8,128)}), f32[96,2048]{1,0:T(8,128)}) %reduce-scatter.2.cloned.1.call-update) | async-done | bytes 786448 | tf_op jit(solution)/shard_map/reduce_scatter | solution.py:77
  157.5 1.4 reshape.311
  158.8 6.6 %gather_fusion.1 = bf16[24,2048,64]{1,2,0:T(8,128)(2,1)} fusion(bf16[16,2048,64]{1,2,0:T(8,128)(2,1)} %bitcast.19, s32[1024]{0:T(1024)S(1)} %pad_clamp_fusion), kind=kCustom, calls=%fused_computation.1 | custom fusion | bytes 12583008 | tf_op jit(solution)/shard_map/gather | solution.py:103
  165.5 4.5 %fusion.39 = f32[24,4,64]{2,1,0:T(4,128)S(1)} fusion(bf16[24,4,2048]{2,1,0:T(4,128)(2,1)S(1)} %reshape.352, bf16[24,2048,64]{1,2,0:T(8,128)(2,1)} %gather_fusion.1), kind=kOutput, calls=%fused_computation.73 | convolution fusion | flops 25165824 | bytes 6709248 | tf_op jit(solution)/shard_map/rsh,rhk->rsk/dot_general | solution.py:105
  170.0 3.6 %psum.7 = f32[24,4,64]{2,1,0:T(4,128)S(1)} all-reduce(f32[24,4,64]{2,1,0:T(4,128)S(1)} %fusion.39), channel_id=1, replica_groups=mesh['rep'=2,'store'=8,'tensor'=2] {'tensor'}, use_global_device_ids=true, to_apply=%region_9.10 | all-reduce | flops 6144 | bytes 49152 | tf_op jit(solution)/shard_map/psum | solution.py:108
  173.6 45.1 %all-to-all-done.2 = bf16[8,2,64,2048]{3,2,1,0:T(8,128)(2,1)} async-done(((bf16[8,2,64,2048]{3,2,1,0:T(8,128)(2,1)}), bf16[8,2,64,2048]{3,2,1,0:T(8,128)(2,1)}, u32[]{:S(2)}, u32[]{:S(2)}) %all-to-all-start.2) | async-done | bytes 4194336 | tf_op jit(solution)/shard_map/all_to_all | solution.py:100
  218.7 6.8 %gather_fusion.3 = bf16[24,64,2048]{2,1,0:T(8,128)(2,1)} fusion(bf16[16,64,2048]{2,1,0:T(8,128)(2,1)} %bitcast.24, s32[1024]{0:T(1024)S(1)} %pad_clamp_fusion), kind=kCustom, calls=%fused_computation.3 | custom fusion | bytes 12583008 | tf_op jit(solution)/shard_map/gather | solution.py:104
  225.5 4.5 %fusion.9 = bf16[24,4,2048]{2,1,0:T(4,128)(2,1)} fusion(f32[24,4,2048]{2,1,0:T(4,128)S(1)} %reshape.311, bf16[24,64,2048]{2,1,0:T(8,128)(2,1)} %gather_fusion.3, f32[24,4,64]{2,1,0:T(4,128)S(1)} %psum.7, f32[24,64]{1,0:T(8,128)S(1)} %fusion.32), kind=kOutput, calls=%fused_computation.16 | convolution fusion | flops 25964544 | bytes 7501824 | tf_op jit(solution)/shard_map/hpx,hxg->hpg/dot_general | solution.py:112
  (41 shorter events, 2.0 us)
Async XLA Ops:
  6.5 15.5 %copy-start = (bf16[8,2048,64]{1,2,0:T(8,128)(2,1)S(1)}, bf16[8,2048,64]{1,2,0:T(8,128)(2,1)}, u32[]{:S(2)}) copy-start(bf16[8,2048,64]{1,2,0:T(8,128)(2,1)} %param.18) | copy-start | bytes 6291460
  24.8 4.7 %copy-start.2 = (bf16[8,64,2048]{2,1,0:T(8,128)(2,1)S(1)}, bf16[8,64,2048]{2,1,0:T(8,128)(2,1)}, u32[]{:S(2)}) copy-start(bf16[8,64,2048]{2,1,0:T(8,128)(2,1)} %param.19) | copy-start | bytes 6291460
  24.8 96.7 %all-to-all-start.1 = ((bf16[8,2,2048,64]{2,3,1,0:T(8,128)(2,1)}), bf16[8,2,2048,64]{2,3,1,0:T(8,128)(2,1)}, u32[]{:S(2)}, u32[]{:S(2)}) async-start(bf16[8,2,2048,64]{2,3,1,0:T(8,128)(2,1)} %bitcast.82), calls=%async_computation.2 | async-start | bytes 8388608 | tf_op jit(solution)/shard_map/all_to_all | solution.py:99
  121.5 4.8 %copy-start.4 = (bf16[2,24,4,2,128]{4,3,2,1,0:T(2,128)(2,1)S(1)}, bf16[2,24,4,2,128]{4,3,2,1,0:T(2,128)(2,1)}, u32[]{:S(2)}) copy-start(bf16[2,24,4,2,128]{4,3,2,1,0:T(2,128)(2,1)} %param.12) | copy-start | bytes 294916
  121.5 4.8 %copy-start.3 = (bf16[24,4,16,128]{3,2,1,0:T(8,128)(2,1)S(1)}, bf16[24,4,16,128]{3,2,1,0:T(8,128)(2,1)}, u32[]{:S(2)}) copy-start(bf16[24,4,16,128]{3,2,1,0:T(8,128)(2,1)} %param.10) | copy-start | bytes 1179652
  121.5 8.0 %copy-start.5 = (s32[24]{0:T(128)S(1)}, s32[24]{0:T(128)}, u32[]{:S(2)}) copy-start(s32[24]{0:T(128)} %param.13) | copy-start | bytes 292
  121.5 97.2 %all-to-all-start.2 = ((bf16[8,2,64,2048]{3,2,1,0:T(8,128)(2,1)}), bf16[8,2,64,2048]{3,2,1,0:T(8,128)(2,1)}, u32[]{:S(2)}, u32[]{:S(2)}) async-start(bf16[8,2,64,2048]{3,2,1,0:T(8,128)(2,1)} %bitcast.83), calls=%async_computation.3 | async-start | bytes 8388608 | tf_op jit(solution)/shard_map/all_to_all | solution.py:100
  126.2 31.3 %reduce-scatter.2.cloned.1.call-start = ((), (), s32[]{:S(2)}) async-start(), calls=%async_computation.4 | async-start | bytes 2359296 | tf_op jit(solution)/shard_map/reduce_scatter | solution.py:77
  218.7 11.3 %copy-start.1 = (bf16[8,2048,64]{1,2,0:T(8,128)(2,1)S(1)}, bf16[8,2048,64]{1,2,0:T(8,128)(2,1)}, u32[]{:S(2)}) copy-start(bf16[8,2048,64]{1,2,0:T(8,128)(2,1)} %param.18) | copy-start | bytes 6291460
Sparse Core Ops, SparseCore 0:
  147.1 10.3 reduce-scatter.1
where the time goes:
time: 237 us
  waiting for transfers between devices  144 us (61%)
  matrix products  26.3 us (11%)
  local copies, waits for them, and re-layouts  22.4 us (9%)
  blocking collectives  17.1 us (7%)
  between operations  13.6 us (6%)
  starting transfers between devices  9.44 us (4%)
  other arithmetic  3.6 us (2%)
    all_to_all x1, waiting for transfers between devices, local(): lax.all_to_all(a_store[asked], 'store', split_axis=0, concat_axis=0, tile...  89.1 us
    all_to_all x1, waiting for transfers between devices, local(): lax.all_to_all(b_store[asked], 'store', split_axis=0, concat_axis=0, tile...  45.1 us
    all_to_all x1, blocking collectives, local(): lax.all_to_all(wanted, 'store', split_axis=0, concat_axis=0, tiled=True)  13.5 us
    reduce_scatter x1, waiting for transfers between devices, local(): lax.psum_scatter(partial_out, 'tensor', scatter_dimension=1, tiled=True)  10.1 us
    dot_general x1, matrix products, local(): jnp.dot(attended.reshape(request_count * step_count, feature_half), w_out...  9.69 us
    gather x1, local copies, waits for them, and re-layouts, local(): got_second.reshape(owners * ACAP, rank_width, out_half)[flat_index]  6.79 us
    gather x1, local copies, waits for them, and re-layouts, local(): got_first.reshape(owners * ACAP, feature_half, rank_width)[flat_index]  6.64 us
  transfers between devices with their start and end apart: 3, of which 3 were waited for; matrix products, arithmetic and copies ran while one was open for 15% of the time, Pallas kernels for 0%

commit v1 on v0

--- a/solution.py
+++ b/solution.py
@@ -5,7 +5,7 @@
 from jax import lax
 from jax.sharding import PartitionSpec as P
 
-ACAP = 2
+QCAP = 3
 
 
 adapter_scale = 8.0
@@ -65,10 +65,34 @@
 
 def local(queries, kv_cache, new_kv, lengths, adapter_ids, place, ranks, w_out, a_store, b_store):
     request_count, step_count = (queries.shape[0], queries.shape[1])
+    owners = lax.axis_size("store")
+    per_owner, feature_half, rank_width = a_store.shape
+    out_half = b_store.shape[2]
+    location = lookup(place, adapter_ids)
+    owner_of = location // per_owner
+    slot_of = location % per_owner
+    order_index = jnp.arange(request_count, dtype=jnp.int32)
+    earlier = order_index[None, :] < order_index[:, None]
+    same_owner = owner_of[:, None] == owner_of[None, :]
+    turn = jnp.sum(same_owner & earlier, axis=1)
+    seat = owner_of * QCAP + turn
+    seats = owners * QCAP
+    pick = seat[:, None] == jnp.arange(seats, dtype=jnp.int32)[None, :]
+    slot_sent = jnp.sum(jnp.where(pick, slot_of[:, None], 0), axis=0)
+    pick = pick.astype(jnp.bfloat16)
+
     attended = attend(queries, kv_cache, new_kv, lengths)
-    feature_half = attended.shape[2]
-    out_half = b_store.shape[2]
-    rank_width = a_store.shape[2]
+    sent = jnp.einsum(
+        "rq,rsf->qsf", pick, attended, preferred_element_type=jnp.float32
+    ).astype(jnp.bfloat16)
+    sent = sent.reshape(owners, QCAP * step_count * feature_half // 128, 128)
+    note = jnp.broadcast_to(
+        slot_sent.reshape(owners, QCAP, 1), (owners, QCAP, 128)
+    ).astype(jnp.bfloat16)
+    note = jnp.pad(note, ((0, 0), (0, 16 - QCAP), (0, 0)))
+    sent = jnp.concatenate([sent, note], axis=1)
+    got = lax.all_to_all(sent, "store", split_axis=0, concat_axis=0, tiled=True)
+
     partial_out = jnp.dot(
         attended.reshape(request_count * step_count, feature_half),
         w_out,
@@ -76,43 +100,29 @@
     )
     plain_projection_sum = lax.psum_scatter(
         partial_out, "tensor", scatter_dimension=1, tiled=True
-    ).reshape(request_count, step_count, out_half)
-    owners = lax.axis_size("store")
-    per_owner = a_store.shape[0]
-    location = lookup(place, adapter_ids)
-    request_rank = lookup(ranks, adapter_ids)
-    owner_of = location // per_owner
-    slot_of = location % per_owner
-    order_index = jnp.arange(request_count, dtype=jnp.int32)
-    earlier = order_index[None, :] < order_index[:, None]
-    same_owner = owner_of[:, None] == owner_of[None, :]
-    owner_range = jnp.arange(owners, dtype=jnp.int32)
-    same_loc = location[:, None] == location[None, :]
-    leading = jnp.logical_not(jnp.any(same_loc & earlier, axis=1))
-    lead_rank = jnp.sum(same_owner & earlier & leading[None, :], axis=1)
-    fetch_col = jnp.sum(jnp.where(same_loc & leading[None, :], lead_rank[None, :], 0), axis=1)
-    hits = leading[:, None, None] & (owner_of[:, None, None] == owner_range[None, :, None])
-    hits = hits & (lead_rank[:, None, None] == jnp.arange(ACAP, dtype=jnp.int32)[None, None, :])
-    wanted = jnp.sum(jnp.where(hits, slot_of[:, None, None], 0), axis=0)
-    asked = lax.all_to_all(wanted, "store", split_axis=0, concat_axis=0, tiled=True)
-    got_first, got_second = (
-        lax.all_to_all(a_store[asked], "store", split_axis=0, concat_axis=0, tiled=True),
-        lax.all_to_all(b_store[asked], "store", split_axis=0, concat_axis=0, tiled=True),
     )
-    flat_index = owner_of * ACAP + fetch_col
-    first_req = got_first.reshape(owners * ACAP, feature_half, rank_width)[flat_index]
-    second_request = got_second.reshape(owners * ACAP, rank_width, out_half)[flat_index]
-    partial_value = jnp.einsum(
-        "rsh,rhk->rsk", attended, first_req, preferred_element_type=jnp.float32
+
+    body = QCAP * step_count * feature_half // 128
+    rows = got[:, :body].reshape(seats * step_count, feature_half)
+    slots = got[:, body : body + QCAP, 0].astype(jnp.int32).reshape(seats)
+    mine = slots[:, None] == jnp.arange(per_owner, dtype=jnp.int32)[None, :]
+    mine = jnp.repeat(mine, step_count, axis=0)
+    here = lax.axis_index("store") * per_owner + jnp.arange(per_owner, dtype=jnp.int32)
+    slot_rank = jnp.sum(jnp.where(here[:, None] == place[None, :], ranks[None, :], 0), axis=1)
+    factor = rank_factor(slot_rank, rank_width)
+    every = jnp.einsum("mf,pfk->mpk", rows, a_store, preferred_element_type=jnp.float32)
+    partial_value = jnp.sum(jnp.where(mine[:, :, None], every, 0.0), axis=1)
+    summed = lax.psum(partial_value, "tensor")
+    spread = jnp.where(mine[:, :, None], summed[:, None, :] * factor[None], 0.0).astype(jnp.bfloat16)
+    update = jnp.einsum(
+        "mpk,pkg->mg", spread, b_store, preferred_element_type=jnp.float32
+    ).astype(jnp.bfloat16)
+    back = lax.all_to_all(
+        update.reshape(owners, body, 128), "store", split_axis=0, concat_axis=0, tiled=True
     )
-    summed = lax.psum(partial_value, "tensor")
-    narrow_product = (summed * rank_factor(request_rank, rank_width)[:, None, :]).astype(
-        jnp.bfloat16
-    )
-    adapter_update = jnp.einsum(
-        "hpx,hxg->hpg", narrow_product, second_request, preferred_element_type=jnp.float32
-    ).astype(jnp.bfloat16)
-    adapter_update = adapter_update.astype(jnp.float32)
+    back = back.reshape(seats, step_count, out_half)
+    adapter_update = jnp.einsum("rq,qsg->rsg", pick, back, preferred_element_type=jnp.float32)
+    plain_projection_sum = plain_projection_sum.reshape(request_count, step_count, out_half)
     return (plain_projection_sum + adapter_update).astype(jnp.bfloat16)
 
 

time: 237 us -> 87.3 us (0.37)
  waiting for transfers between devices: 144 us -> 12.1 us
  local copies, waits for them, and re-layouts: 22.4 us -> 6.96 us
  matrix products: 26.3 us -> 22.5 us
    all_to_all x2 -> x1, waiting for transfers between devices: 134 us -> 12.1 us  [local(): got = lax.all_to_all(sent, 'store', split_axis=0, concat_axis=0, tiled=True)]
    gather x4 -> x0, local copies, waits for them, and re-layouts: 19.1 us -> none  [the longest x1 6.79 us: local(): got_second.reshape(owners * ACAP, rank_width, out_half)[flat_index]]
    reduce_scatter x1, waiting for transfers between devices: 10.1 us -> 0.02 us  [local(): lax.psum_scatter(partial_out, 'tensor', scatter_dimension=1, tiled=True)]
    dot_general x2 -> x3, matrix products: 8.96 us -> 3.49 us  [the longest x1 2.18 us: local(): jnp.einsum('mpk,pkg->mg', spread, b_store, preferred_element_type=jnp.flo...]
    all_to_all x1, blocking collectives: 13.5 us -> 16 us  [local(): lax.all_to_all(update.reshape(owners, body, 128), 'store', split_axis=0,...]
    all_to_all x2 -> x1, starting transfers between devices: 9.4 us -> 7.28 us  [local(): got = lax.all_to_all(sent, 'store', split_axis=0, concat_axis=0, tiled=True)]
  transfers between devices with their start and end apart: 3 -> 2, of which waited for: 3 -> 1; matrix products, arithmetic and copies ran while one was open for 15% -> 8% of each run, Pallas kernels for 0% -> 0%
where the time goes in v1:
time: 87.3 us; the launch traced here: 86.8 us
  matrix products  22.5 us (26%)
  blocking collectives  19.4 us (22%)
  between operations  13.6 us (16%)
  waiting for transfers between devices  12.1 us (14%)
  starting transfers between devices  7.29 us (8%)
  local copies, waits for them, and re-layouts  6.96 us (8%)
  other arithmetic  4.86 us (6%)
    all_to_all x1, blocking collectives, local(): lax.all_to_all(update.reshape(owners, body, 128), 'store', split_axis=0,...  16 us
    all_to_all x1, waiting for transfers between devices, local(): got = lax.all_to_all(sent, 'store', split_axis=0, concat_axis=0, tiled=True)  12.1 us
    dot_general x1, matrix products, local(): jnp.dot(attended.reshape(request_count * step_count, feature_half), w_out...  9.69 us
    all_to_all x1, starting transfers between devices, local(): got = lax.all_to_all(sent, 'store', split_axis=0, concat_axis=0, tiled=True)  7.28 us
    psum x1, blocking collectives, local(): summed = lax.psum(partial_value, 'tensor')  3.41 us
    dot_general x1, matrix products, attend(): jnp.einsum('rsngd,rncd->rsngc', grouped, kv_cache[0], preferred_element_t...  3.12 us
    dot_general x1, matrix products, attend(): jnp.einsum('rsngd,rtnd->rsngt', grouped, new_kv[0], preferred_element_typ...  2.81 us
    dot_general x1, matrix products, attend(): jnp.einsum('rsngc,rncd->rsngd', weights_bf[..., :cache_slots], kv_cache[1...  2.5 us
  transfers between devices with their start and end apart: 2, of which 1 were waited for; matrix products, arithmetic and copies ran while one was open for 8% of the time, Pallas kernels for 0%

profile of v1, /device:TPU:0, one launch (start us, length us, event | category | flops | bytes accessed | tf_op | source)
XLA Modules:
  0.0 86.8 jit_solution(12610553416740635604)
XLA Ops:
  6.5 1.1 %fusion.43 = (bf16[1,24,4,2,128]{4,3,2,1,0:T(2,128)(2,1)S(1)}, bf16[1,24,4,2,128]{4,3,2,1,0:T(2,128)(2,1)S(1)}) fusion(bf16[2,24,4,2,128]{4,3,2,1,0:T(2,128)(2,1)} %param.12), kind=kLoop, calls=%fused_computation.65 | loop fusion | bytes 196608 | tf_op jit(solution)/shard_map/slice | solution.py:60
  7.6 2.8 %fusion.27 = f32[24,2,4,4,8]{4,2,3,1,0:T(4,128)S(1)} fusion(bf16[1,24,4,2,128]{4,3,2,1,0:T(2,128)(2,1)S(1)} %get-tuple-element.8, bf16[24,4,16,128]{3,2,1,0:T(8,128)(2,1)} %param.10), kind=kOutput, calls=%fused_computation.26 | convolution fusion | flops 1572864 | bytes 466944 | tf_op jit(solution)/shard_map/rsngd,rtnd->rsngt/dot_general | solution.py:42
  10.4 0.3 copy.82
  10.9 1.3 %iota_compare_fusion.1 = pred[24,256]{1,0:T(8,128)(4,1)} fusion(s32[24]{0:T(128)} %param.13), kind=kLoop, calls=%fused_computation.38 | loop fusion | flops 6144 | bytes 6240 | tf_op jit(solution)/shard_map/lt | solution.py:39
  12.2 0.8 copy.83
  13.1 3.1 %fusion.44 = (f32[24,4,2,8]{3,1,2,0:T(4,128)S(1)}, f32[24,4,2,8,256]{4,3,1,2,0:T(8,128)S(1)}) fusion(bf16[2,24,2,256,128]{4,3,2,1,0:T(8,128)(2,1)} %param.11, pred[24,256]{1,0:T(8,128)(4,1)} %iota_compare_fusion.1, bf16[24,4,16,128]{3,2,1,0:T(8,128)(2,1)S(1)} %copy-done.1), kind=kOutput, calls=%fused_computation.66 | convolution fusion | flops 101841408 | bytes 5124096 | tf_op jit(solution)/shard_map/rsngd,rncd->rsngc/dot_general | solution.py:36
  16.3 0.9 %fusion.9 = f32[24,4,2,8]{3,1,2,0:T(4,128)S(1)} fusion(f32[24,4,2,8,4]{4,3,1,2,0:T(8,128)S(1)} %copy.83, f32[24,4,2,8,256]{4,3,1,2,0:T(8,128)S(1)} %get-tuple-element.12, f32[24,4,2,8]{3,1,2,0:T(4,128)S(1)} %reduce_max.22), kind=kLoop, calls=%fused_computation.14 | loop fusion | flops 1196544 | bytes 1609728 | tf_op jit(solution)/shard_map/reduce_sum | solution.py:50
  17.2 0.6 divide_convert_fusion
  18.1 2.5 %fusion.18 = bf16[24,4,2,8,128]{4,3,1,2,0:T(8,128)(2,1)S(1)} fusion(f32[24,2,4,8,128]{4,3,2,1,0:T(8,128)S(1)} %fusion.24, bf16[2,24,2,256,128]{4,3,2,1,0:T(8,128)(2,1)} %param.11, bf16[24,4,2,8,260]{4,3,1,2,0:T(8,128)(2,1)S(1)} %divide_convert_fusion), kind=kOutput, calls=%fused_computation.18 | convolution fusion | flops 101056512 | bytes 5111808 | tf_op jit(solution)/shard_map/rsngc,rncd->rsngd/dot_general | solution.py:51
  20.8 9.7 %fusion.45 = f32[96,4096]{1,0:T(8,128)} fusion(bf16[96,2048]{1,0:T(8,128)(2,1)S(1)} %convert_element_type.62, bf16[2048,4096]{1,0:T(8,128)(2,1)} %param.17), kind=kOutput, calls=%fused_computation.67 | convolution fusion | flops 1610612736 | bytes 18743296 | tf_op jit(solution)/shard_map/dot_general | solution.py:96
  30.8 0.4 copy-done.3
  31.6 0.4 convolution_convert_fusion
  32.0 0.3 copy.90
  32.3 0.2 reshape.170
  32.8 0.8 fusion.23
  33.6 7.3 %all-to-all-start = ((bf16[8,208,128]{2,1,0:T(8,128)(2,1)}), bf16[8,208,128]{2,1,0:T(8,128)(2,1)S(1)}, u32[]{:S(2)}, u32[]{:S(2)}) async-start(bf16[8,208,128]{2,1,0:T(8,128)(2,1)} %fusion.23), calls=%async_computation.1 | async-start | bytes 851968 | tf_op jit(solution)/shard_map/all_to_all | solution.py:94
  41.2 12.1 %all-to-all-done = bf16[8,208,128]{2,1,0:T(8,128)(2,1)S(1)} async-done(((bf16[8,208,128]{2,1,0:T(8,128)(2,1)}), bf16[8,208,128]{2,1,0:T(8,128)(2,1)S(1)}, u32[]{:S(2)}, u32[]{:S(2)}) %all-to-all-start) | async-done | bytes 426016 | tf_op jit(solution)/shard_map/all_to_all | solution.py:94
  54.0 0.7 fusion.46
  54.7 3.4 %psum.7 = f32[96,64]{0,1:T(8,128)S(1)} all-reduce(f32[96,64]{0,1:T(8,128)S(1)} %select_reduce_fusion), channel_id=1, replica_groups=mesh['rep'=2,'store'=8,'tensor'=2] {'tensor'}, use_global_device_ids=true, to_apply=%region_8.9 | all-reduce | flops 6144 | bytes 49152 | tf_op jit(solution)/shard_map/psum | solution.py:115
  58.2 2.2 %fusion.8 = bf16[96,2048]{1,0:T(8,128)(2,1)S(1)} fusion(bf16[8,64,2048]{2,1,0:T(8,128)(2,1)} %param.19, f32[8,64]{1,0:T(8,128)S(1)} %fusion.40, f32[96,64]{0,1:T(8,128)S(1)} %psum.7, pred[96,8]{0,1:T(8,128)(4,1)S(1)} %copy.91), kind=kOutput, calls=%fused_computation.12 | convolution fusion | flops 201670656 | bytes 2517760 | tf_op jit(solution)/shard_map/mpk,pkg->mg/dot_general | solution.py:117
  60.5 16.0 %all_to_all.10 = bf16[8,192,128]{2,1,0:T(8,128)(2,1)S(1)} all-to-all(bf16[8,192,128]{2,1,0:T(8,128)(2,1)S(1)} %reshape.172), channel_id=1, replica_groups=mesh['rep'=2,'store'=8,'tensor'=2] {'store'}, dimensions={0} | all-to-all | bytes 786432 | tf_op jit(solution)/shard_map/all_to_all | solution.py:120
  76.6 1.4 %reshape.169 = f32[24,4,2048]{2,1,0:T(4,128)S(1)} reshape(f32[96,2048]{1,0:T(8,128)} %reduce-scatter.2.cloned.1.call-done) | data formatting | bytes 1572864 | tf_op jit(solution)/shard_map/reshape | solution.py:125
  78.0 0.9 %fusion.7 = bf16[24,4,2048]{2,0,1:T(8,128)(2,1)S(1)} fusion(f32[24,4,2048]{2,1,0:T(4,128)S(1)} %reshape.169, bf16[24,4,2048]{2,1,0:T(4,128)(2,1)S(1)} %reshape.173, s32[24]{0:T(128)S(1)} %multiply_add_fusion), kind=kOutput, calls=%fused_computation.11 | convolution fusion | flops 9830976 | bytes 1572960 | tf_op jit(solution)/shard_map/rq,qsg->rsg/dot_general | solution.py:124
  78.9 1.1 %copy.94 = bf16[24,4,2048]{2,1,0:T(4,128)(2,1)} copy(bf16[24,4,2048]{2,0,1:T(8,128)(2,1)S(1)} %fusion.7) | data formatting | bytes 786432 | tf_op jit(solution)/shard_map/convert_element_type | solution.py:126
  (43 shorter events, 2.9 us)
Async XLA Ops:
  6.5 47.4 %copy-start = (bf16[8,2048,64]{1,2,0:T(8,128)(2,1)S(1)}, bf16[8,2048,64]{1,2,0:T(8,128)(2,1)}, u32[]{:S(2)}) copy-start(bf16[8,2048,64]{1,2,0:T(8,128)(2,1)} %param.18) | copy-start | bytes 6291460
  6.5 6.6 %copy-start.1 = (bf16[24,4,16,128]{3,2,1,0:T(8,128)(2,1)S(1)}, bf16[24,4,16,128]{3,2,1,0:T(8,128)(2,1)}, u32[]{:S(2)}) copy-start(bf16[24,4,16,128]{3,2,1,0:T(8,128)(2,1)} %param.10) | copy-start | bytes 1179652
  6.5 70.1 %reduce-scatter.2.cloned.1.call-start = ((), (), s32[]{:S(2)}) async-start(), calls=%async_computation.3 | async-start | bytes 2359296 | tf_op jit(solution)/shard_map/reduce_scatter | solution.py:101
  30.5 0.7 copy-start.3
  30.5 0.7 copy-start.4
  30.6 10.3 %copy-start.2 = (s32[64]{0:T(128)S(1)}, s32[64]{0:T(128)}, u32[]{:S(2)}) copy-start(s32[64]{0:T(128)} %param.16) | copy-start | bytes 772
  33.6 19.7 %all-to-all-start = ((bf16[8,208,128]{2,1,0:T(8,128)(2,1)}), bf16[8,208,128]{2,1,0:T(8,128)(2,1)S(1)}, u32[]{:S(2)}, u32[]{:S(2)}) async-start(bf16[8,208,128]{2,1,0:T(8,128)(2,1)} %fusion.23), calls=%async_computation.1 | async-start | bytes 851968 | tf_op jit(solution)/shard_map/all_to_all | solution.py:94
Sparse Core Ops, SparseCore 0:
  30.7 11.7 reduce-scatter.1

commit v2 on v1

--- a/solution.py
+++ b/solution.py
@@ -93,14 +93,22 @@
     sent = jnp.concatenate([sent, note], axis=1)
     got = lax.all_to_all(sent, "store", split_axis=0, concat_axis=0, tiled=True)
 
+    held, _ = lax.optimization_barrier((attended, sent))
     partial_out = jnp.dot(
-        attended.reshape(request_count * step_count, feature_half),
+        held.reshape(request_count * step_count, feature_half),
         w_out,
         preferred_element_type=jnp.float32,
     )
-    plain_projection_sum = lax.psum_scatter(
-        partial_out, "tensor", scatter_dimension=1, tiled=True
-    )
+    got, partial_out = lax.optimization_barrier((got, partial_out))
+    core = lax.axis_index("tensor")
+    cores = lax.axis_size("tensor")
+    plain_projection_sum = lax.dynamic_slice_in_dim(partial_out, core * out_half, out_half, 1)
+    for step in range(1, cores):
+        target = (core + step) % cores
+        share = lax.dynamic_slice_in_dim(partial_out, target * out_half, out_half, 1)
+        plain_projection_sum = plain_projection_sum + lax.ppermute(
+            share, "tensor", [(k, (k + step) % cores) for k in range(cores)]
+        )
 
     body = QCAP * step_count * feature_half // 128
     rows = got[:, :body].reshape(seats * step_count, feature_half)
@@ -112,7 +120,11 @@
     factor = rank_factor(slot_rank, rank_width)
     every = jnp.einsum("mf,pfk->mpk", rows, a_store, preferred_element_type=jnp.float32)
     partial_value = jnp.sum(jnp.where(mine[:, :, None], every, 0.0), axis=1)
-    summed = lax.psum(partial_value, "tensor")
+    summed = partial_value
+    for step in range(1, cores):
+        summed = summed + lax.ppermute(
+            partial_value, "tensor", [(k, (k + step) % cores) for k in range(cores)]
+        )
     spread = jnp.where(mine[:, :, None], summed[:, None, :] * factor[None], 0.0).astype(jnp.bfloat16)
     update = jnp.einsum(
         "mpk,pkg->mg", spread, b_store, preferred_element_type=jnp.float32

time: 87.3 us -> 63.7 us (0.73)
  blocking collectives: 19.4 us -> 0 us
  between operations: 13.6 us -> 0.28 us
  starting transfers between devices: 7.29 us -> 11.4 us
  waiting for transfers between devices: 12.1 us -> 14.3 us
  local copies, waits for them, and re-layouts: 6.96 us -> 8.77 us
  other arithmetic: 4.86 us -> 6.33 us
    all_to_all x1 -> x0, blocking collectives: 16 us -> none  [local(): lax.all_to_all(update.reshape(owners, body, 128), 'store', split_axis=0,...]
    all_to_all x0 -> x1, waiting for transfers between devices: none -> 12.3 us  [local(): lax.all_to_all(update.reshape(owners, body, 128), 'store', split_axis=0,...]
    all_to_all x1, waiting for transfers between devices: 12.1 us -> 1.98 us  [local(): got = lax.all_to_all(sent, 'store', split_axis=0, concat_axis=0, tiled=True)]
    all_to_all x0 -> x1, starting transfers between devices: none -> 4.02 us  [local(): lax.all_to_all(update.reshape(owners, body, 128), 'store', split_axis=0,...]
    psum x1 -> x0, blocking collectives: 3.41 us -> none  [local(): summed = lax.psum(partial_value, 'tensor')]
    dot_general x1, matrix products: 2.18 us -> 0.59 us  [local(): jnp.einsum('mpk,pkg->mg', spread, b_store, preferred_element_type=jnp.flo...]
    add x0 -> x2, other arithmetic: none -> 1.47 us  [the longest x1 1.46 us: local(): plain_projection_sum + lax.ppermute(share, 'tensor', [(k, (k + step) % co...]
    dot_general x1, matrix products: 0.93 us -> 2.07 us  [local(): jnp.einsum('rq,qsg->rsg', pick, back, preferred_element_type=jnp.float32)]
  transfers between devices with their start and end apart: 2 -> 4, of which waited for: 1 -> 2; matrix products, arithmetic and copies ran while one was open for 8% -> 20% of each run, Pallas kernels for 0% -> 0%
where the time goes in v2:
time: 63.7 us; the launch traced here: 63.2 us
  matrix products  22.1 us (35%)
  waiting for transfers between devices  14.3 us (22%)
  starting transfers between devices  11.4 us (18%)
  local copies, waits for them, and re-layouts  8.77 us (14%)
  other arithmetic  6.33 us (10%)
    all_to_all x1, waiting for transfers between devices, local(): lax.all_to_all(update.reshape(owners, body, 128), 'store', split_axis=0,...  12.3 us
    dot_general x1, matrix products, local(): jnp.dot(held.reshape(request_count * step_count, feature_half), w_out, pr...  9.7 us
    all_to_all x1, starting transfers between devices, local(): got = lax.all_to_all(sent, 'store', split_axis=0, concat_axis=0, tiled=True)  7.28 us
    all_to_all x1, starting transfers between devices, local(): lax.all_to_all(update.reshape(owners, body, 128), 'store', split_axis=0,...  4.02 us
    dot_general x1, matrix products, attend(): jnp.einsum('rsngd,rncd->rsngc', grouped, kv_cache[0], preferred_element_t...  3.12 us
    dot_general x1, matrix products, attend(): jnp.einsum('rsngd,rtnd->rsngt', grouped, new_kv[0], preferred_element_typ...  2.81 us
    dot_general x1, matrix products, attend(): jnp.einsum('rsngc,rncd->rsngd', weights_bf[..., :cache_slots], kv_cache[1...  2.5 us
    dot_general x1, matrix products, local(): jnp.einsum('rq,qsg->rsg', pick, back, preferred_element_type=jnp.float32)  2.07 us
  transfers between devices with their start and end apart: 4, of which 2 were waited for; matrix products, arithmetic and copies ran while one was open for 20% of the time, Pallas kernels for 0%

profile of v2, /device:TPU:0, one launch (start us, length us, event | category | flops | bytes accessed | tf_op | source)
XLA Modules:
  0.0 63.2 jit_solution(7738808484439170566)
XLA Ops:
  0.0 1.1 %fusion.46 = (bf16[1,24,4,2,128]{4,3,2,1,0:T(2,128)(2,1)S(1)}, bf16[1,24,4,2,128]{4,3,2,1,0:T(2,128)(2,1)S(1)}) fusion(bf16[2,24,4,2,128]{4,3,2,1,0:T(2,128)(2,1)} %param.12), kind=kLoop, calls=%fused_computation.68 | loop fusion | bytes 196608 | tf_op jit(solution)/shard_map/slice | solution.py:60
  1.1 2.8 %fusion.30 = f32[24,2,4,4,8]{4,2,3,1,0:T(4,128)S(1)} fusion(bf16[1,24,4,2,128]{4,3,2,1,0:T(2,128)(2,1)S(1)} %get-tuple-element.14, bf16[24,4,16,128]{3,2,1,0:T(8,128)(2,1)} %param.10), kind=kOutput, calls=%fused_computation.28 | convolution fusion | flops 1572864 | bytes 466944 | tf_op jit(solution)/shard_map/rsngd,rtnd->rsngt/dot_general | solution.py:42
  4.4 1.3 %iota_compare_fusion.1 = pred[24,256]{1,0:T(8,128)(4,1)} fusion(s32[24]{0:T(128)} %param.13), kind=kLoop, calls=%fused_computation.40 | loop fusion | flops 6144 | bytes 6240 | tf_op jit(solution)/shard_map/lt | solution.py:39
  5.7 0.8 %copy.84 = f32[24,4,2,8,4]{4,3,1,2,0:T(8,128)S(1)} copy(f32[24,4,2,8,4]{0,3,1,4,2:T(8,128)S(1)} %get-tuple-element.12) | data formatting | bytes 49152 | tf_op jit(solution)/shard_map/jit(_where)/select_n | solution.py:46
  6.6 3.1 %fusion.47 = (f32[24,4,2,8]{3,1,2,0:T(4,128)S(1)}, f32[24,4,2,8,256]{4,3,1,2,0:T(8,128)S(1)}) fusion(bf16[2,24,2,256,128]{4,3,2,1,0:T(8,128)(2,1)} %param.11, pred[24,256]{1,0:T(8,128)(4,1)} %iota_compare_fusion.1, bf16[24,4,16,128]{3,2,1,0:T(8,128)(2,1)S(1)} %copy-done.3), kind=kOutput, calls=%fused_computation.69 | convolution fusion | flops 101841408 | bytes 5124096 | tf_op jit(solution)/shard_map/rsngd,rncd->rsngc/dot_general | solution.py:36
  9.7 0.9 %fusion.8 = f32[24,4,2,8]{3,1,2,0:T(4,128)S(1)} fusion(f32[24,4,2,8,4]{4,3,1,2,0:T(8,128)S(1)} %copy.84, f32[24,4,2,8,256]{4,3,1,2,0:T(8,128)S(1)} %get-tuple-element.18, f32[24,4,2,8]{3,1,2,0:T(4,128)S(1)} %reduce_max.22), kind=kLoop, calls=%fused_computation.12 | loop fusion | flops 1196544 | bytes 1609728 | tf_op jit(solution)/shard_map/reduce_sum | solution.py:50
  10.6 0.6 %divide_convert_fusion = bf16[24,4,2,8,260]{4,3,1,2,0:T(8,128)(2,1)S(1)} fusion(f32[24,4,2,8,4]{4,3,1,2,0:T(8,128)S(1)} %copy.84, f32[24,4,2,8,256]{4,3,1,2,0:T(8,128)S(1)} %get-tuple-element.18, f32[24,4,2,8]{3,1,2,0:T(4,128)S(1)} %fusion.8, f32[24,4,2,8]{3,1,2,0:T(4,128)S(1)} %reduce_max.22), kind=kLoop, calls=%fused_computation.9 | loop fusion | flops 1597440 | bytes 2408448 | tf_op jit(solution)/shard_map/convert_element_type | solution.py:50
  11.6 2.5 %fusion.17 = bf16[24,4,2,8,128]{4,3,1,2,0:T(8,128)(2,1)S(1)} fusion(f32[24,2,4,8,128]{4,3,2,1,0:T(8,128)S(1)} %fusion.24, bf16[2,24,2,256,128]{4,3,2,1,0:T(8,128)(2,1)} %param.11, bf16[24,4,2,8,260]{4,3,1,2,0:T(8,128)(2,1)S(1)} %divide_convert_fusion), kind=kOutput, calls=%fused_computation.16 | convolution fusion | flops 101056512 | bytes 5111808 | tf_op jit(solution)/shard_map/rsngc,rncd->rsngd/dot_general | solution.py:51
  14.7 0.4 convolution_convert_fusion
  16.0 0.8 %fusion.23 = bf16[8,208,128]{2,1,0:T(8,128)(2,1)} fusion(bf16[8,3,128]{2,1,0:T(4,128)(2,1)S(1)} %broadcast_in_dim.133, bf16[8,192,128]{2,1,0:T(8,128)(2,1)S(1)} %reshape.169), kind=kLoop, calls=%fused_computation.23 | loop fusion | flops 1277952 | bytes 825344 | tf_op jit(solution)/shard_map/concatenate | solution.py:93
  16.8 7.3 %all-to-all-start = ((bf16[8,208,128]{2,1,0:T(8,128)(2,1)}), bf16[8,208,128]{2,1,0:T(8,128)(2,1)S(1)}, u32[]{:S(2)}, u32[]{:S(2)}) async-start(bf16[8,208,128]{2,1,0:T(8,128)(2,1)} %fusion.23), calls=%async_computation | async-start | bytes 851968 | tf_op jit(solution)/shard_map/all_to_all | solution.py:94
  24.8 9.7 %fusion.48 = f32[96,4096]{1,0:T(8,128)} fusion(bf16[96,2048]{1,0:T(8,128)(2,1)S(1)} %reshape.170, bf16[2048,4096]{1,0:T(8,128)(2,1)} %param.17), kind=kOutput, calls=%fused_computation.70 | convolution fusion | flops 1610612736 | bytes 18743296 | tf_op jit(solution)/shard_map/dot_general | solution.py:97
  34.5 2.0 %all-to-all-done = bf16[8,208,128]{2,1,0:T(8,128)(2,1)S(1)} async-done(((bf16[8,208,128]{2,1,0:T(8,128)(2,1)}), bf16[8,208,128]{2,1,0:T(8,128)(2,1)S(1)}, u32[]{:S(2)}, u32[]{:S(2)}) %all-to-all-start) | async-done | bytes 426016 | tf_op jit(solution)/shard_map/all_to_all | solution.py:94
  37.1 0.7 %fusion.49 = f32[96,512]{0,1:S(1)} fusion(bf16[96,2048]{1,0:T(8,128)(2,1)S(1)} %reshape.172, bf16[2048,512]{0,1:T(8,128)(2,1)S(1)} %bitcast.72), kind=kOutput, calls=%fused_computation.71 | convolution fusion | flops 201326592 | bytes 2686976
  38.0 0.6 copy-done.1
  38.5 0.9 %constant_dynamic-slice_fusion = f32[96,2048]{1,0:T(8,128)} fusion(f32[96,4096]{1,0:T(8,128)S(1)} %copy-done.1, s32[]{:T(128)S(6)} %select_n.86), kind=kLoop, calls=%fused_computation.65 | loop fusion | bytes 1572868 | tf_op jit(solution)/shard_map/dynamic_slice | solution.py:108
  39.5 0.6 fusion.7
  40.1 0.9 %reshape.173 = bf16[8,192,128]{2,1,0:T(8,128)(2,1)} reshape(bf16[96,2048]{1,0:T(8,128)(2,1)S(1)} %fusion.7) | data formatting | bytes 786432 | tf_op jit(solution)/shard_map/reshape | solution.py:133
  41.0 4.0 %all-to-all-start.1 = ((bf16[8,192,128]{2,1,0:T(8,128)(2,1)}), bf16[8,192,128]{2,1,0:T(8,128)(2,1)S(1)}, u32[]{:S(2)}, u32[]{:S(2)}) async-start(bf16[8,192,128]{2,1,0:T(8,128)(2,1)} %reshape.173), calls=%async_computation.1 | async-start | bytes 786432 | tf_op jit(solution)/shard_map/all_to_all | solution.py:132
  45.1 12.3 %all-to-all-done.1 = bf16[8,192,128]{2,1,0:T(8,128)(2,1)S(1)} async-done(((bf16[8,192,128]{2,1,0:T(8,128)(2,1)}), bf16[8,192,128]{2,1,0:T(8,128)(2,1)S(1)}, u32[]{:S(2)}, u32[]{:S(2)}) %all-to-all-start.1) | async-done | bytes 393248 | tf_op jit(solution)/shard_map/all_to_all | solution.py:132
  57.5 1.5 %dynamic-slice_add_fusion = f32[96,2048]{1,0:T(8,128)S(1)} fusion(f32[96,2048]{1,0:T(8,128)} %collective-permute-done, f32[96,4096]{1,0:T(8,128)} %fusion.48, s32[]{:T(128)S(6)} %select_n.84), kind=kLoop, calls=%fused_computation.22 | loop fusion | flops 196608 | bytes 2359300 | tf_op jit(solution)/shard_map/add | solution.py:109
  59.0 1.1 %reshape.171 = f32[24,4,2048]{2,1,0:T(4,128)} reshape(f32[96,2048]{1,0:T(8,128)S(1)} %dynamic-slice_add_fusion) | data formatting | bytes 1572864 | tf_op jit(solution)/shard_map/reshape | solution.py:137
  60.1 2.1 %fusion.22 = bf16[24,4,2048]{2,0,1:T(8,128)(2,1)S(1)} fusion(f32[24,4,2048]{2,1,0:T(4,128)} %reshape.171, bf16[24,4,2048]{2,1,0:T(4,128)(2,1)S(1)} %reshape.174, s32[24]{0:T(128)S(1)} %multiply_add_fusion), kind=kOutput, calls=%fused_computation.21 | convolution fusion | flops 9830976 | bytes 1572960 | tf_op jit(solution)/shard_map/rq,qsg->rsg/dot_general | solution.py:136
  62.1 1.1 %copy.95 = bf16[24,4,2048]{2,1,0:T(4,128)(2,1)} copy(bf16[24,4,2048]{2,0,1:T(8,128)(2,1)S(1)} %fusion.22) | data formatting | bytes 786432 | tf_op jit(solution)/shard_map/convert_element_type | solution.py:138
  (51 shorter events, 3.8 us)
Async XLA Ops:
  0.0 37.1 %copy-start = (bf16[8,2048,64]{1,2,0:T(8,128)(2,1)S(1)}, bf16[8,2048,64]{1,2,0:T(8,128)(2,1)}, u32[]{:S(2)}) copy-start(bf16[8,2048,64]{1,2,0:T(8,128)(2,1)} %param.18) | copy-start | bytes 6291460
  0.0 6.6 %copy-start.3 = (bf16[24,4,16,128]{3,2,1,0:T(8,128)(2,1)S(1)}, bf16[24,4,16,128]{3,2,1,0:T(8,128)(2,1)}, u32[]{:S(2)}) copy-start(bf16[24,4,16,128]{3,2,1,0:T(8,128)(2,1)} %param.10) | copy-start | bytes 1179652
  11.5 2.8 %copy-start.5 = (s32[64]{0:T(128)S(1)}, s32[64]{0:T(128)}, u32[]{:S(2)}) copy-start(s32[64]{0:T(128)} %param.15) | copy-start | bytes 772
  11.6 2.8 %copy-start.6 = (s32[24]{0:T(128)S(1)}, s32[24]{0:T(128)}, u32[]{:S(2)}) copy-start(s32[24]{0:T(128)} %param.14) | copy-start | bytes 292
  15.1 9.4 %copy-start.4 = (s32[64]{0:T(128)S(1)}, s32[64]{0:T(128)}, u32[]{:S(2)}) copy-start(s32[64]{0:T(128)} %param.16) | copy-start | bytes 772
  16.8 19.7 %all-to-all-start = ((bf16[8,208,128]{2,1,0:T(8,128)(2,1)}), bf16[8,208,128]{2,1,0:T(8,128)(2,1)S(1)}, u32[]{:S(2)}, u32[]{:S(2)}) async-start(bf16[8,208,128]{2,1,0:T(8,128)(2,1)} %fusion.23), calls=%async_computation | async-start | bytes 851968 | tf_op jit(solution)/shard_map/all_to_all | solution.py:94
  37.1 1.4 %copy-start.1 = (f32[96,4096]{1,0:T(8,128)S(1)}, f32[96,4096]{1,0:T(8,128)}, u32[]{:S(2)}) copy-start(f32[96,4096]{1,0:T(8,128)} %fusion.48) | copy-start | bytes 4718596
  37.1 2.4 %copy-start.2 = (bf16[8,64,2048]{2,1,0:T(8,128)(2,1)S(1)}, bf16[8,64,2048]{2,1,0:T(8,128)(2,1)}, u32[]{:S(2)}) copy-start(bf16[8,64,2048]{2,1,0:T(8,128)(2,1)} %param.19) | copy-start | bytes 6291460
  37.9 1.6 %collective-permute-start.1 = (f32[96,64]{0,1:T(8,128)S(1)}, f32[96,64]{0,1:T(8,128)S(1)}, u32[]{:S(2)}, u32[]{:S(2)}) collective-permute-start(f32[96,64]{0,1:T(8,128)S(1)} %select_reduce_fusion), channel_id=1, source_target_pairs={{0,1},{1,0},{2,3},{3,2},{4,5},{5,4},{6,7},{7,6},{8,9},{9,8},{10,11... | collective-permute-start | bytes 73736 | tf_op jit(solution)/shard_map/ppermute | solution.py:125
  39.5 18.0 %collective-permute-start = (f32[96,2048]{1,0:T(8,128)}, f32[96,2048]{1,0:T(8,128)}, u32[]{:S(2)}, u32[]{:S(2)}) collective-permute-start(f32[96,2048]{1,0:T(8,128)} %constant_dynamic-slice_fusion), channel_id=1, source_target_pairs={{0,1},{1,0},{2,3},{3,2},{4,5},{5,4},{6,7},{7,6},{8,9},{9,8},{10,11... | collective-permute-start | bytes 2359304 | tf_op jit(solution)/shard_map/ppermute | solution.py:109
  41.0 16.4 %all-to-all-start.1 = ((bf16[8,192,128]{2,1,0:T(8,128)(2,1)}), bf16[8,192,128]{2,1,0:T(8,128)(2,1)S(1)}, u32[]{:S(2)}, u32[]{:S(2)}) async-start(bf16[8,192,128]{2,1,0:T(8,128)(2,1)} %reshape.173), calls=%async_computation.1 | async-start | bytes 786432 | tf_op jit(solution)/shard_map/all_to_all | solution.py:132

commit v3 on v1

v3 whole, which is shorter than its diff:
```python
import functools
import math

import jax
import jax.numpy as jnp
from jax import lax
from jax.experimental import pallas as pl
from jax.experimental.pallas import tpu as pltpu
from jax.sharding import PartitionSpec as P

QCAP = 3
LANES = 128
NOTE = 16
ATTEND_VMEM = 60 * 1024 * 1024
SMALL_VMEM = 8 * 1024 * 1024
BATCH = 4

adapter_scale = 8.0


def rank_factor(request_rank, width):
    column_indices = jnp.arange(width, dtype=jnp.int32)
    rank_as_real = request_rank.astype(jnp.float32)[..., None]
    return jnp.where(
        column_indices < request_rank[..., None], adapter_scale / jnp.sqrt(rank_as_real), 0.0
    )


def dot(left, right, contract=(1, 0)):
    return lax.dot_general(
        left, right, (((contract[0],), (contract[1],)), ((), ())), preferred_element_type=jnp.float32
    )


def attend_kernel(
    steps, heads, per_owner,
    lengths, adapter_ids, place,
    q_ref, kv_ref, new_ref,
    attended_ref, sent_ref, seat_ref,
    taken, slots,
):
    owners = taken.shape[0]
    seats = owners * QCAP
    requests = seat_ref.shape[0]
    batch, rows, width = q_ref.shape
    slots_in_cache = kv_ref.shape[3]
    group = heads // 2
    step = pl.program_id(0)

    @pl.when(step == 0)
    def _():
        for owner in range(owners):
            taken[owner] = 0
        for seat in range(seats):
            slots[seat] = 0
        if seats > requests:
            sent_ref[...] = jnp.zeros_like(sent_ref)

    row = lax.broadcasted_iota(jnp.int32, (rows, width), 0)
    first = (row // group) % 2 == 0
    new_count = new_ref.shape[2]
    new_row = lax.broadcasted_iota(jnp.int32, (rows, new_count), 0)
    new_column = lax.broadcasted_iota(jnp.int32, (rows, new_count), 1)
    new_seen = (new_column // 2 <= new_row // heads) & (new_column % 2 == (new_row // group) % 2)
    column = lax.broadcasted_iota(jnp.int32, (rows, slots_in_cache), 1)
    scale = 1.0 / math.sqrt(width)

    cached, fresh = [], []
    for j in range(batch):
        q = q_ref[j]
        q_wide = q.astype(jnp.float32)
        both = jnp.concatenate(
            [jnp.where(first, q_wide, 0.0), jnp.where(first, 0.0, q_wide)], axis=1
        ).astype(jnp.bfloat16)
        keys = jnp.concatenate([kv_ref[0, j, 0], kv_ref[0, j, 1]], axis=1)
        scores = dot(both, keys, (1, 1)) * scale
        cached.append(jnp.where(column < lengths[step * batch + j], scores, -jnp.inf))
        scores = dot(q, new_ref[0, j], (1, 1)) * scale
        fresh.append(jnp.where(new_seen, scores, -jnp.inf))
    tops = [
        jnp.maximum(jnp.max(a, axis=1, keepdims=True), jnp.max(b, axis=1, keepdims=True))
        for a, b in zip(cached, fresh)
    ]
    cached = [jnp.exp(a - top) for a, top in zip(cached, tops)]
    fresh = [jnp.exp(b - top) for b, top in zip(fresh, tops)]
    sums = [
        1.0 / (jnp.sum(a, axis=1, keepdims=True) + jnp.sum(b, axis=1, keepdims=True))
        for a, b in zip(cached, fresh)
    ]
    cached = [(a * inv).astype(jnp.bfloat16) for a, inv in zip(cached, sums)]
    fresh = [(b * inv).astype(jnp.bfloat16) for b, inv in zip(fresh, sums)]
    for j in range(batch):
        values = jnp.concatenate([kv_ref[1, j, 0], kv_ref[1, j, 1]], axis=1)
        both = dot(cached[j], values)
        result = jnp.where(first, both[:, :width], both[:, width:]) + dot(fresh[j], new_ref[1, j])
        result = result.astype(jnp.bfloat16)
        request = step * batch + j
        location = place[adapter_ids[request]]
        owner = location // per_owner
        turn = taken[owner]
        taken[owner] = turn + 1
        slots[owner * QCAP + turn] = location % per_owner
        seat_ref[request] = owner * QCAP + turn
        attended_ref[j] = result
        sent_ref[owner, pl.ds(pl.multiple_of(turn * rows, rows), rows), :] = result

    @pl.when(step == steps - 1)
    def _():
        note_row = lax.broadcasted_iota(jnp.int32, (NOTE, width), 0)
        per_seat = rows // heads
        for owner in range(owners):
            note = jnp.zeros((NOTE, width), jnp.int32)
            for turn in range(QCAP):
                note = jnp.where(note_row // per_seat == turn, slots[owner * QCAP + turn], note)
            sent_ref[owner, QCAP * rows :, :] = note.astype(jnp.float32).astype(jnp.bfloat16)


def attend(queries, kv_cache, new_kv, lengths, adapter_ids, place, owners, per_owner):
    requests, step_count, heads, width = queries.shape
    cache_slots = kv_cache.shape[3]
    rows = step_count * heads
    new_rows = new_kv.shape[2] * new_kv.shape[3]
    batch = BATCH if requests % BATCH == 0 else 1
    steps = requests // batch
    body = QCAP * rows + NOTE
    return pl.pallas_call(
        functools.partial(attend_kernel, steps, heads, per_owner),
        grid_spec=pltpu.PrefetchScalarGridSpec(
            num_scalar_prefetch=3,
            grid=(steps,),
            in_specs=[
                pl.BlockSpec((batch, rows, width), lambda i, *_: (i, 0, 0)),
                pl.BlockSpec((2, batch, 2, cache_slots, width), lambda i, *_: (0, i, 0, 0, 0)),
                pl.BlockSpec((2, batch, new_rows, width), lambda i, *_: (0, i, 0, 0)),
            ],
            out_specs=[
                pl.BlockSpec((batch, rows, width), lambda i, *_: (i, 0, 0)),
                pl.BlockSpec((owners, body, width), lambda i, *_: (0, 0, 0)),
                pl.BlockSpec(memory_space=pltpu.SMEM),
            ],
            scratch_shapes=[
                pltpu.SMEM((owners,), jnp.int32),
                pltpu.SMEM((owners * QCAP,), jnp.int32),
            ],
        ),
        out_shape=[
            jax.ShapeDtypeStruct((requests, rows, width), jnp.bfloat16),
            jax.ShapeDtypeStruct((owners, body, width), jnp.bfloat16),
            jax.ShapeDtypeStruct((requests,), jnp.int32),
        ],
        compiler_params=pltpu.CompilerParams(
            dimension_semantics=("arbitrary",), vmem_limit_bytes=ATTEND_VMEM
        ),
        cost_estimate=pl.CostEstimate(
            flops=4 * requests * rows * cache_slots * width * 2,
            bytes_accessed=kv_cache.size * 2 + 4 * queries.size,
            transcendentals=requests * rows * cache_slots,
        ),
        name="attend",
    )(
        lengths,
        adapter_ids,
        place,
        queries.reshape(requests, rows, width),
        kv_cache,
        new_kv.reshape(2, requests, new_rows, width),
    )


def low_kernel(seats, steps, got_ref, a_ref, low_ref, slot_ref, wide):
    owners, rows, width = got_ref.shape
    body = rows - NOTE
    per_owner, rank_width, features = a_ref.shape
    for owner in range(owners):
        wide[owner * body : (owner + 1) * body, :] = got_ref[owner, :body, :].astype(jnp.float32)
    blocks = features // width
    total = seats * steps
    x = jnp.concatenate(
        [wide[pl.ds(c, total, stride=blocks), :].astype(jnp.bfloat16) for c in range(blocks)], axis=1
    )
    per_group = total // owners
    for owner in range(owners):
        slot_ref[owner * per_group : (owner + 1) * per_group, :] = got_ref[owner, body:, :].astype(
            jnp.float32
        )[:per_group]
    every = dot(x, a_ref[...].reshape(per_owner * rank_width, features), (1, 1))
    slot = slot_ref[...].astype(jnp.int32)
    lane = lax.broadcasted_iota(jnp.int32, (total, width), 1)
    per_block = width // rank_width
    kept = jnp.zeros((total, width), jnp.float32)
    for c in range(per_owner // per_block):
        mine = slot == c * per_block + lane // rank_width
        kept = kept + jnp.where(mine, every[:, c * width : (c + 1) * width], 0.0)
    folded = kept
    for k in range(1, per_block):
        folded = folded + pltpu.roll(kept, k * rank_width, 1)
    low_ref[...] = folded


def low(got, a_turned, seats, steps):
    owners, rows, width = got.shape
    total = seats * steps
    return pl.pallas_call(
        functools.partial(low_kernel, seats, steps),
        out_shape=[
            jax.ShapeDtypeStruct((total, width), jnp.float32),
            jax.ShapeDtypeStruct((total, width), jnp.float32),
        ],
        in_specs=[pl.BlockSpec(memory_space=pltpu.VMEM)] * 2,
        out_specs=[pl.BlockSpec(memory_space=pltpu.VMEM)] * 2,
        scratch_shapes=[pltpu.VMEM((owners * (rows - NOTE), width), jnp.float32)],
        compiler_params=pltpu.CompilerParams(vmem_limit_bytes=SMALL_VMEM),
        cost_estimate=pl.CostEstimate(
            flops=2 * total * a_turned.size, bytes_accessed=2 * a_turned.size, transcendentals=0
        ),
        name="low",
    )(got, a_turned)


def update_kernel(own_ref, other_ref, slot_ref, factor_ref, b_ref, back_ref, wide):
    total, width = own_ref.shape
    per_owner, rank_width, columns = b_ref.shape
    owners, body, _ = back_ref.shape
    summed = own_ref[...]
    for k in range(other_ref.shape[0]):
        summed = summed + other_ref[k]
    slot = slot_ref[...].astype(jnp.int32)
    lane = lax.broadcasted_iota(jnp.int32, (total, width), 1)
    per_block = width // rank_width
    spread = []
    for c in range(per_owner // per_block):
        mine = slot == c * per_block + lane // rank_width
        scaled = summed * factor_ref[:, c * width : (c + 1) * width]
        spread.append(jnp.where(mine, scaled, 0.0).astype(jnp.bfloat16))
    spread = jnp.concatenate(spread, axis=1)
    result = dot(spread, b_ref[...].reshape(per_owner * rank_width, columns))
    blocks = columns // width
    for c in range(blocks):
        wide[pl.ds(c, total, stride=blocks), :] = result[:, c * width : (c + 1) * width]
    for owner in range(owners):
        back_ref[owner] = wide[owner * body : (owner + 1) * body, :].astype(jnp.bfloat16)


def update(own, others, slot, factor, b_store, owners):
    total, width = own.shape
    columns = b_store.shape[2]
    body = total * columns // width // owners
    return pl.pallas_call(
        update_kernel,
        out_shape=jax.ShapeDtypeStruct((owners, body, width), jnp.bfloat16),
        in_specs=[pl.BlockSpec(memory_space=pltpu.VMEM)] * 5,
        out_specs=pl.BlockSpec(memory_space=pltpu.VMEM),
        scratch_shapes=[pltpu.VMEM((owners * body, width), jnp.float32)],
        compiler_params=pltpu.CompilerParams(vmem_limit_bytes=SMALL_VMEM),
        cost_estimate=pl.CostEstimate(
            flops=2 * total * b_store.size, bytes_accessed=2 * b_store.size, transcendentals=0
        ),
        name="update",
    )(own, others, slot, factor, b_store)


def finish_kernel(seat, core, back_ref, base_ref, other_ref, out_ref, wide):
    requests, steps, columns = out_ref.shape
    owners, body, width = back_ref.shape
    rows = body // QCAP
    blocks = columns // width
    total = requests * steps
    for request in range(requests):
        owner = seat[request] // QCAP
        turn = seat[request] % QCAP
        wide[request * rows : (request + 1) * rows, :] = back_ref[
            owner, pl.ds(pl.multiple_of(turn * rows, rows), rows), :
        ].astype(jnp.float32)
    for c in range(blocks):
        here = slice(c * width, (c + 1) * width)
        mixed = base_ref[:, here]
        for k in range(other_ref.shape[0]):
            mixed = mixed + other_ref[k, :, here].astype(jnp.float32)
        mixed = mixed + wide[pl.ds(c, total, stride=blocks), :]
        out_ref[:, :, here] = mixed.reshape(requests, steps, width).astype(out_ref.dtype)


def finish(seat, core, back, partial_out, others, requests, steps, columns):
    owners, body, width = back.shape
    total = requests * steps
    return pl.pallas_call(
        finish_kernel,
        grid_spec=pltpu.PrefetchScalarGridSpec(
            num_scalar_prefetch=2,
            grid=(1,),
            in_specs=[
                pl.BlockSpec(back.shape, lambda i, seat, core: (0, 0, 0)),
                pl.BlockSpec((total, columns), lambda i, seat, core: (0, core[0])),
                pl.BlockSpec(others.shape, lambda i, seat, core: (0, 0, 0)),
            ],
            out_specs=pl.BlockSpec((requests, steps, columns), lambda i, seat, core: (0, 0, 0)),
            scratch_shapes=[pltpu.VMEM((requests * body // QCAP, width), jnp.float32)],
        ),
        out_shape=jax.ShapeDtypeStruct((requests, steps, columns), jnp.bfloat16),
        compiler_params=pltpu.CompilerParams(vmem_limit_bytes=SMALL_VMEM),
        cost_estimate=pl.CostEstimate(
            flops=3 * total * columns, bytes_accessed=12 * total * columns, transcendentals=0
        ),
        name="finish",
    )(seat, core, back, partial_out, others)


def local(queries, kv_cache, new_kv, lengths, adapter_ids, place, ranks, w_out, a_store, b_store):
    request_count, step_count = (queries.shape[0], queries.shape[1])
    owners = lax.axis_size("store")
    cores = lax.axis_size("tensor")
    core = lax.axis_index("tensor")
    per_owner, feature_half, rank_width = a_store.shape
    out_half = b_store.shape[2]
    seats = owners * QCAP
    shifts = [[(k, (k + step) % cores) for k in range(cores)] for step in range(1, cores)]

    attended, sent, seat = attend(
        queries, kv_cache, new_kv, lengths, adapter_ids, place, owners, per_owner
    )
    got = lax.all_to_all(sent, "store", split_axis=0, concat_axis=0, tiled=True)

    partial_out = jnp.dot(
        attended.reshape(request_count * step_count, feature_half),
        w_out,
        preferred_element_type=jnp.float32,
    )
    here = lax.axis_index("store") * per_owner + jnp.arange(per_owner, dtype=jnp.int32)
    slot_rank = jnp.sum(jnp.where(here[:, None] == place[None, :], ranks[None, :], 0), axis=1)
    factor = rank_factor(slot_rank, rank_width).reshape(1, per_owner * rank_width)

    got, partial_out = lax.optimization_barrier((got, partial_out))
    own, slot = low(got, jnp.swapaxes(a_store, 1, 2), seats, step_count)
    others = jnp.stack([lax.ppermute(own, "tensor", shift) for shift in shifts])
    back = update(own, others, slot, factor, b_store, owners)
    back, partial_out = lax.optimization_barrier((back, partial_out))
    back = lax.all_to_all(back, "store", split_axis=0, concat_axis=0, tiled=True)

    shares = []
    for step, shift in enumerate(shifts, 1):
        target = (core + step) % cores
        share = lax.dynamic_slice_in_dim(partial_out, target * out_half, out_half, 1)
        shares.append(lax.ppermute(share, "tensor", shift))
    return finish(
        seat, core.reshape(1), back, partial_out, jnp.stack(shares), request_count, step_count, out_half
    )


def solution(mesh):
    return jax.shard_map(
        local,
        mesh=mesh,
        in_specs=(
            P(("rep", "store"), None, "tensor", None),
            P(None, ("rep", "store"), "tensor", None, None),
            P(None, ("rep", "store"), None, "tensor", None),
            P(("rep", "store")),
            P(("rep", "store")),
            P("rep"),
            P("rep"),
            P("tensor", None),
            P(("rep", "store"), "tensor", None),
            P(("rep", "store"), None, "tensor"),
        ),
        out_specs=P(("rep", "store"), None, "tensor"),
        check_vma=False,
    )
```

time: 87.3 us -> 52.6 us (0.60)
  matrix products: 22.5 us -> 8.55 us
  between operations: 13.6 us -> 0.07 us
  Pallas kernels: 0 us -> 11.6 us
  waiting for transfers between devices: 12.1 us -> 3.49 us
  other arithmetic: 4.86 us -> 0.27 us
  blocking collectives: 19.4 us -> 16 us
  local copies, waits for them, and re-layouts: 6.96 us -> 4.5 us
    dot_general x7 -> x0, matrix products: 12.2 us -> none  [the longest x1 3.12 us: attend(): jnp.einsum('rsngd,rncd->rsngc', grouped, kv_cache[0], preferred_element_t...]
    pallas_call x0 -> x4, Pallas kernels: none -> 11.6 us  [the longest x1 8.32 us: attend(): pl.pallas_call(functools.partial(attend_kernel, steps, heads, per_owner),...]
    all_to_all x1, waiting for transfers between devices: 12.1 us -> 2.42 us  [local(): got = lax.all_to_all(sent, 'store', split_axis=0, concat_axis=0, tiled=True)]
    psum x1 -> x0, blocking collectives: 3.41 us -> none  [local(): summed = lax.psum(partial_value, 'tensor')]
    unnamed x10, local copies, waits for them, and re-layouts: 0.39 us -> 3.19 us
    convert_element_type x8 -> x0, local copies, waits for them, and re-layouts: 2.01 us -> none  [the longest x1 1.05 us: local(): return (plain_projection_sum + adapter_update).astype(jnp.bfloat16)]
    reduce_sum x5 -> x0, other arithmetic: 1.4 us -> none  [the longest x1 0.91 us: attend(): jnp.sum(exponent, axis=-1, keepdims=True)]
    lt x1 -> x0, other arithmetic: 1.32 us -> none  [attend(): jnp.arange(cache_slots, dtype=jnp.int32)[None, :] < lengths[:, None]]
  transfers between devices with their start and end apart: 2 -> 3, of which waited for: 1 -> 2; matrix products, arithmetic and copies ran while one was open for 8% -> 19% of each run, Pallas kernels for 0% -> 0%
where the time goes in v3:
time: 52.6 us; the launch traced here: 52.1 us
  blocking collectives  16 us (30%)
  Pallas kernels  11.6 us (22%)
  matrix products  8.55 us (16%)
  starting transfers between devices  7.59 us (14%)
  local copies, waits for them, and re-layouts  4.5 us (9%)
  waiting for transfers between devices  3.49 us (7%)
    all_to_all x1, blocking collectives, local(): lax.all_to_all(back, 'store', split_axis=0, concat_axis=0, tiled=True)  16 us
    dot_general x1, matrix products, local(): jnp.dot(attended.reshape(request_count * step_count, feature_half), w_out...  8.55 us
    pallas_call x1, Pallas kernels, attend(): pl.pallas_call(functools.partial(attend_kernel, steps, heads, per_owner),...  8.32 us
    all_to_all x1, starting transfers between devices, local(): got = lax.all_to_all(sent, 'store', split_axis=0, concat_axis=0, tiled=True)  7.29 us
    unnamed x10, local copies, waits for them, and re-layouts  3.19 us
    all_to_all x1, waiting for transfers between devices, local(): got = lax.all_to_all(sent, 'store', split_axis=0, concat_axis=0, tiled=True)  2.42 us
    pallas_call x1, Pallas kernels, finish(): pl.pallas_call(finish_kernel, grid_spec=pltpu.PrefetchScalarGridSpec(num_...  1.84 us
    reshape x1, local copies, waits for them, and re-layouts, local(): attended.reshape(request_count * step_count, feature_half)  1.17 us
  transfers between devices with their start and end apart: 3, of which 2 were waited for; matrix products, arithmetic and copies ran while one was open for 19% of the time, Pallas kernels for 0%

profile of v3, /device:TPU:0, one launch (start us, length us, event | category | flops | bytes accessed | tf_op | source)
XLA Modules:
  0.0 52.1 jit_solution(14237938423227925538)
XLA Ops:
  0.0 0.0 copy-start.3
  0.0 8.3 %attend.1 = (bf16[24,64,128]{2,1,0:T(8,128)(2,1)}, bf16[8,208,128]{2,1,0:T(8,128)(2,1)}, s32[24]{0:T(128)}) custom-call(s32[24]{0:T(128)} %lengths.1, s32[24]{0:T(128)} %adapter_ids.1, s32[64]{0:T(128)} %place.1, bf16[24,64,128]{2,1,0:T(8,128)(2,1)} %bitcast.11, bf16[2,24,2,256,128]{4,3,2,1,0:T(8,128)(2,1)} %kv_ref.1, bf16[2,24,8,128]{3,2,1,0:T(8,128)(2,1)} %bitcast.12), custom_call_target="tpu_custom_call" | custom-call | flops 402653184 | bytes 7077888 | tf_op jit(solution)/shard_map/attend/pallas_call | solution.py:126
  8.3 7.3 %all-to-all-start = ((bf16[8,208,128]{2,1,0:T(8,128)(2,1)}), bf16[8,208,128]{2,1,0:T(8,128)(2,1)S(1)}, u32[]{:S(2)}, u32[]{:S(2)}) async-start(bf16[8,208,128]{2,1,0:T(8,128)(2,1)} %get-tuple-element.15), calls=%async_computation | async-start | bytes 851968 | tf_op jit(solution)/shard_map/all_to_all | solution.py:321
  15.6 0.0 copy-done.3
  15.6 0.0 copy-done.4
  15.6 0.2 select_reduce_fusion
  15.8 1.2 %reshape.66 = bf16[96,2048]{1,0:T(8,128)(2,1)S(1)} reshape(bf16[24,64,128]{2,1,0:T(8,128)(2,1)} %get-tuple-element.16) | data formatting | bytes 786432 | tf_op jit(solution)/shard_map/reshape | solution.py:324
  17.0 8.6 %fusion.1.base_ref = f32[96,4096]{1,0:T(8,128)S(1)} fusion(bf16[96,2048]{1,0:T(8,128)(2,1)S(1)} %reshape.66, bf16[2048,4096]{1,0:T(8,128)(2,1)} %param.17), kind=kOutput, calls=%fused_computation.6 | convolution fusion | flops 1610612736 | bytes 18743296 | tf_op jit(solution)/shard_map/dot_general | solution.py:323
  25.6 0.0 copy-start.2
  25.6 2.4 %all-to-all-done.got_ref = bf16[8,208,128]{2,1,0:T(8,128)(2,1)S(1)} async-done(((bf16[8,208,128]{2,1,0:T(8,128)(2,1)}), bf16[8,208,128]{2,1,0:T(8,128)(2,1)S(1)}, u32[]{:S(2)}, u32[]{:S(2)}) %all-to-all-start) | async-done | bytes 426016 | tf_op jit(solution)/shard_map/all_to_all | solution.py:321
  28.0 1.6 %copy-done = bf16[8,2048,64]{1,2,0:T(8,128)(2,1)S(1)} copy-done((bf16[8,2048,64]{1,2,0:T(8,128)(2,1)S(1)}, bf16[8,2048,64]{1,2,0:T(8,128)(2,1)}, u32[]{:S(2)}) %copy-start) | copy-done | bytes 2097176
  29.6 0.9 %low.1 = (f32[96,128]{1,0:T(8,128)S(1)}, f32[96,128]{1,0:T(8,128)S(1)}) custom-call(bf16[8,208,128]{2,1,0:T(8,128)(2,1)S(1)} %all-to-all-done.got_ref, bf16[8,64,2048]{2,1,0:T(8,128)(2,1)S(1)} %bitcast.8), custom_call_target="tpu_custom_call" | custom-call | flops 201326592 | bytes 2097152 | tf_op jit(solution)/shard_map/low/pallas_call | solution.py:203
  30.5 0.1 collective-permute-start
  30.6 0.1 fusion
  30.6 0.1 select_n.30.factor_ref
  30.7 1.1 %collective-permute-done = f32[96,128]{1,0:T(8,128)S(1)} collective-permute-done((f32[96,128]{1,0:T(8,128)S(1)}, f32[96,128]{1,0:T(8,128)S(1)}, u32[]{:S(2)}, u32[]{:S(2)}) %collective-permute-start) | collective-permute-done | bytes 49184 | tf_op jit(solution)/shard_map/ppermute | solution.py:334
  31.8 1.6 %copy-done.1 = bf16[8,64,2048]{2,1,0:T(8,128)(2,1)S(1)} copy-done((bf16[8,64,2048]{2,1,0:T(8,128)(2,1)S(1)}, bf16[8,64,2048]{2,1,0:T(8,128)(2,1)}, u32[]{:S(2)}) %copy-start.1) | copy-done | bytes 2097176
  33.4 0.6 %update.1 = bf16[8,192,128]{2,1,0:T(8,128)(2,1)S(1)} custom-call(f32[96,128]{1,0:T(8,128)S(1)} %get-tuple-element.18.own_ref, f32[1,96,128]{2,1,0:T(8,128)S(1)} %bitcast.10, f32[96,128]{1,0:T(8,128)S(1)} %get-tuple-element.19.slot_ref, f32[1,512]{1,0:T(1,128)S(1)} %select_n.30.factor_ref, bf16[8,64,2048]{2,1,0:T(8,128)(2,1)S(1)} %copy-done.1), custom_call_target="tpu_custom_call" | custom-call | flops 201326592 | bytes 2097152 | tf_op jit(solution)/shard_map/update/pallas_call | solution.py:248
  34.0 0.1 constant_dynamic-slice_fusion
  34.0 0.2 collective-permute-start.1
  34.3 16.0 %all_to_all.10.back_ref = bf16[8,192,128]{2,1,0:T(8,128)(2,1)S(1)} all-to-all(bf16[8,192,128]{2,1,0:T(8,128)(2,1)S(1)} %update.1), channel_id=1, replica_groups=mesh['rep'=2,'store'=8,'tensor'=2] {'store'}, dimensions={0} | all-to-all | bytes 786432 | tf_op jit(solution)/shard_map/all_to_all | solution.py:337
  50.2 0.0 collective-permute-done.1
  50.2 0.0 copy-done.2
  50.2 1.8 %finish.1 = bf16[24,4,2048]{2,1,0:T(4,128)(2,1)} custom-call(s32[24]{0:T(128)S(1)} %copy-done.2, s32[1]{0:T(128)} %bitcast.2.core, bf16[8,192,128]{2,1,0:T(8,128)(2,1)S(1)} %all_to_all.10.back_ref, f32[96,4096]{1,0:T(8,128)S(1)} %fusion.1.base_ref, f32[1,96,2048]{2,1,0:T(8,128)S(1)} %bitcast.9), custom_call_target="tpu_custom_call" | custom-call | flops 589824 | bytes 2359296 | tf_op jit(solution)/shard_map/finish/pallas_call | solution.py:286
  (5 shorter events, 0.0 us)
Async XLA Ops:
  0.0 15.6 %copy-start.3 = (s32[64]{0:T(128)S(1)}, s32[64]{0:T(128)}, u32[]{:S(2)}) copy-start(s32[64]{0:T(128)} %place.1) | copy-start | bytes 772
  0.0 15.6 %copy-start.4 = (s32[64]{0:T(128)S(1)}, s32[64]{0:T(128)}, u32[]{:S(2)}) copy-start(s32[64]{0:T(128)} %param.16) | copy-start | bytes 772
  8.3 19.7 %all-to-all-start = ((bf16[8,208,128]{2,1,0:T(8,128)(2,1)}), bf16[8,208,128]{2,1,0:T(8,128)(2,1)S(1)}, u32[]{:S(2)}, u32[]{:S(2)}) async-start(bf16[8,208,128]{2,1,0:T(8,128)(2,1)} %get-tuple-element.15), calls=%async_computation | async-start | bytes 851968 | tf_op jit(solution)/shard_map/all_to_all | solution.py:321
  25.6 24.7 %copy-start.2 = (s32[24]{0:T(128)S(1)}, s32[24]{0:T(128)}, u32[]{:S(2)}) copy-start(s32[24]{0:T(128)} %get-tuple-element.14.seat) | copy-start | bytes 292
  28.0 1.6 %copy-start = (bf16[8,2048,64]{1,2,0:T(8,128)(2,1)S(1)}, bf16[8,2048,64]{1,2,0:T(8,128)(2,1)}, u32[]{:S(2)}) copy-start(bf16[8,2048,64]{1,2,0:T(8,128)(2,1)} %param.18) | copy-start | bytes 6291460
  30.5 1.3 %collective-permute-start = (f32[96,128]{1,0:T(8,128)S(1)}, f32[96,128]{1,0:T(8,128)S(1)}, u32[]{:S(2)}, u32[]{:S(2)}) collective-permute-start(f32[96,128]{1,0:T(8,128)S(1)} %get-tuple-element.18.own_ref), channel_id=1, source_target_pairs={{0,1},{1,0},{2,3},{3,2},{4,5},{5,4},{6,7},{7,6},{8,9},{9,8},{10,11... | collective-permute-start | bytes 147464 | tf_op jit(solution)/shard_map/ppermute | solution.py:334
  31.8 1.6 %copy-start.1 = (bf16[8,64,2048]{2,1,0:T(8,128)(2,1)S(1)}, bf16[8,64,2048]{2,1,0:T(8,128)(2,1)}, u32[]{:S(2)}) copy-start(bf16[8,64,2048]{2,1,0:T(8,128)(2,1)} %b_ref.1) | copy-start | bytes 6291460
  34.0 16.2 %collective-permute-start.1 = (f32[96,2048]{1,0:T(8,128)S(1)}, f32[96,2048]{1,0:T(8,128)S(1)}, u32[]{:S(2)}, u32[]{:S(2)}) collective-permute-start(f32[96,2048]{1,0:T(8,128)S(1)} %constant_dynamic-slice_fusion), channel_id=1, source_target_pairs={{0,1},{1,0},{2,3},{3,2},{4,5},{5,4},{6,7},{7,6},{8,9},{9,8},{10,11... | collective-permute-start | bytes 2359304 | tf_op jit(solution)/shard_map/ppermute | solution.py:343

commit v4 on v3

--- a/solution.py
+++ b/solution.py
@@ -11,25 +11,28 @@
 QCAP = 3
 LANES = 128
 NOTE = 16
-ATTEND_VMEM = 60 * 1024 * 1024
-SMALL_VMEM = 8 * 1024 * 1024
-BATCH = 4
+ATTEND_VMEM = 24 * 1024 * 1024
+TILE = 1024
+BASE_VMEM = 32 * 1024 * 1024
+BATCH = 12
+FINISH = 2
+SMALL_VMEM = 16 * 1024 * 1024
 
 adapter_scale = 8.0
-
-
-def rank_factor(request_rank, width):
-    column_indices = jnp.arange(width, dtype=jnp.int32)
-    rank_as_real = request_rank.astype(jnp.float32)[..., None]
-    return jnp.where(
-        column_indices < request_rank[..., None], adapter_scale / jnp.sqrt(rank_as_real), 0.0
-    )
 
 
 def dot(left, right, contract=(1, 0)):
     return lax.dot_general(
         left, right, (((contract[0],), (contract[1],)), ((), ())), preferred_element_type=jnp.float32
     )
+
+
+def far(x):
+    return pltpu.with_memory_space_constraint(x, pltpu.HBM)
+
+
+def near(x):
+    return pltpu.with_memory_space_constraint(x, pltpu.VMEM)
 
 
 def attend_kernel(
@@ -101,7 +104,7 @@
         taken[owner] = turn + 1
         slots[owner * QCAP + turn] = location % per_owner
         seat_ref[request] = owner * QCAP + turn
-        attended_ref[j] = result
+        attended_ref[request] = result
         sent_ref[owner, pl.ds(pl.multiple_of(turn * rows, rows), rows), :] = result
 
     @pl.when(step == steps - 1)
@@ -134,7 +137,7 @@
                 pl.BlockSpec((2, batch, new_rows, width), lambda i, *_: (0, i, 0, 0)),
             ],
             out_specs=[
-                pl.BlockSpec((batch, rows, width), lambda i, *_: (i, 0, 0)),
+                pl.BlockSpec(memory_space=pltpu.VMEM),
                 pl.BlockSpec((owners, body, width), lambda i, *_: (0, 0, 0)),
                 pl.BlockSpec(memory_space=pltpu.SMEM),
             ],
@@ -144,8 +147,8 @@
             ],
         ),
         out_shape=[
-            jax.ShapeDtypeStruct((requests, rows, width), jnp.bfloat16),
-            jax.ShapeDtypeStruct((owners, body, width), jnp.bfloat16),
+            pltpu.VMEM((requests, rows, width), jnp.bfloat16),
+            pltpu.HBM((owners, body, width), jnp.bfloat16),
             jax.ShapeDtypeStruct((requests,), jnp.int32),
         ],
         compiler_params=pltpu.CompilerParams(
@@ -158,13 +161,130 @@
         ),
         name="attend",
     )(
-        lengths,
-        adapter_ids,
-        place,
-        queries.reshape(requests, rows, width),
-        kv_cache,
-        new_kv.reshape(2, requests, new_rows, width),
+        far(lengths),
+        far(adapter_ids),
+        far(place),
+        far(queries.reshape(requests, rows, width)),
+        far(kv_cache),
+        far(new_kv.reshape(2, requests, new_rows, width)),
     )
+
+
+def other_columns_kernel(
+    block, here, place, ranks,
+    attended_ref, w_ref, a_ref,
+    out_ref, x_ref, a_near, factor_ref,
+    wide, arrived,
+):
+    copy = pltpu.make_async_copy(a_ref, a_near, arrived)
+    last = pl.program_id(0) == pl.num_programs(0) - 1
+
+    @pl.when(pl.program_id(0) == 0)
+    def _():
+        total, width = x_ref.shape[0], wide.shape[1]
+        blocks = x_ref.shape[1] // width
+        wide[...] = attended_ref[...].reshape(wide.shape).astype(jnp.float32)
+        for c in range(blocks):
+            x_ref[:, c * width : (c + 1) * width] = wide[pl.ds(c, total, stride=blocks), :].astype(
+                jnp.bfloat16
+            )
+
+    @pl.when(last)
+    def _():
+        copy.start()
+
+    out_ref[...] = dot(x_ref[...], w_ref[...])
+
+    @pl.when(last)
+    def _():
+        rank_width = a_ref.shape[1]
+        part = lax.broadcasted_iota(jnp.int32, factor_ref.shape, 0)
+        lane = lax.broadcasted_iota(jnp.int32, factor_ref.shape, 1)
+        position = here[0] + (part * factor_ref.shape[1] + lane) // rank_width
+        rank = jnp.zeros(factor_ref.shape, jnp.int32)
+        for adapter in range(place.shape[0]):
+            rank = rank + jnp.where(position == place[adapter], ranks[adapter], 0)
+        scale = adapter_scale / jnp.sqrt(rank.astype(jnp.float32))
+        factor_ref[...] = jnp.where(lane % rank_width < rank, scale, 0.0)
+        copy.wait()
+
+
+def other_columns(attended, w_out, block, columns, here, place, ranks, a_turned):
+    requests, rows, width = attended.shape
+    features = w_out.shape[0]
+    total = requests * rows * width // features
+    tile = min(TILE, columns)
+    steps = columns // tile
+    parts = a_turned.shape[0] * a_turned.shape[1] // width
+    whole = pl.BlockSpec(memory_space=pltpu.VMEM)
+    return pl.pallas_call(
+        other_columns_kernel,
+        grid_spec=pltpu.PrefetchScalarGridSpec(
+            num_scalar_prefetch=4,
+            grid=(steps,),
+            in_specs=[
+                whole,
+                pl.BlockSpec((features, tile), lambda i, block, *_: (0, block[0] * steps + i)),
+                pl.BlockSpec(memory_space=pl.ANY),
+            ],
+            out_specs=[
+                pl.BlockSpec((total, tile), lambda i, *_: (0, i)),
+                pl.BlockSpec((total, features), lambda i, *_: (0, 0)),
+                whole,
+                whole,
+            ],
+            scratch_shapes=[
+                pltpu.VMEM((requests * rows, width), jnp.float32),
+                pltpu.SemaphoreType.DMA,
+            ],
+        ),
+        out_shape=[
+            jax.ShapeDtypeStruct((total, columns), jnp.float32),
+            pltpu.HBM((total, features), jnp.bfloat16),
+            pltpu.VMEM(a_turned.shape, a_turned.dtype),
+            pltpu.VMEM((parts, width), jnp.float32),
+        ],
+        compiler_params=pltpu.CompilerParams(
+            dimension_semantics=("arbitrary",), vmem_limit_bytes=BASE_VMEM
+        ),
+        cost_estimate=pl.CostEstimate(
+            flops=2 * total * features * columns,
+            bytes_accessed=2 * features * columns + 4 * a_turned.size,
+            transcendentals=0,
+        ),
+        name="other_columns",
+    )(block, here, far(place), far(ranks), near(attended), far(w_out), far(a_turned))
+
+
+def own_columns_kernel(block, x_ref, w_ref, share_ref, out_ref):
+    out_ref[...] = dot(x_ref[...], w_ref[...]) + share_ref[...]
+
+
+def own_columns(x, w_out, block, columns, share):
+    total, features = x.shape
+    tile = min(TILE, columns)
+    steps = columns // tile
+    return pl.pallas_call(
+        own_columns_kernel,
+        grid_spec=pltpu.PrefetchScalarGridSpec(
+            num_scalar_prefetch=1,
+            grid=(steps,),
+            in_specs=[
+                pl.BlockSpec((total, features), lambda i, block: (0, 0)),
+                pl.BlockSpec((features, tile), lambda i, block: (0, block[0] * steps + i)),
+                pl.BlockSpec((total, tile), lambda i, block: (0, i)),
+            ],
+            out_specs=pl.BlockSpec((total, tile), lambda i, block: (0, i)),
+        ),
+        out_shape=jax.ShapeDtypeStruct((total, columns), jnp.float32),
+        compiler_params=pltpu.CompilerParams(
+            dimension_semantics=("arbitrary",), vmem_limit_bytes=BASE_VMEM
+        ),
+        cost_estimate=pl.CostEstimate(
+            flops=2 * total * features * columns, bytes_accessed=2 * features * columns, transcendentals=0
+        ),
+        name="own_columns",
+    )(block, far(x), far(w_out), share)
 
 
 def low_kernel(seats, steps, got_ref, a_ref, low_ref, slot_ref, wide):
@@ -214,31 +334,40 @@
             flops=2 * total * a_turned.size, bytes_accessed=2 * a_turned.size, transcendentals=0
         ),
         name="low",
-    )(got, a_turned)
-
-
-def update_kernel(own_ref, other_ref, slot_ref, factor_ref, b_ref, back_ref, wide):
+    )(got, near(a_turned))
+
+
+def update_kernel(own_ref, other_ref, slot_ref, factor_ref, b_ref, back_ref, wide, ready, left):
     total, width = own_ref.shape
     per_owner, rank_width, columns = b_ref.shape
     owners, body, _ = back_ref.shape
+    per_block = width // rank_width
+    blocks = columns // width
+    parts = per_owner // per_block
     summed = own_ref[...]
     for k in range(other_ref.shape[0]):
         summed = summed + other_ref[k]
     slot = slot_ref[...].astype(jnp.int32)
     lane = lax.broadcasted_iota(jnp.int32, (total, width), 1)
-    per_block = width // rank_width
     spread = []
-    for c in range(per_owner // per_block):
+    for c in range(parts):
         mine = slot == c * per_block + lane // rank_width
-        scaled = summed * factor_ref[:, c * width : (c + 1) * width]
+        scaled = summed * factor_ref[c : c + 1, :]
         spread.append(jnp.where(mine, scaled, 0.0).astype(jnp.bfloat16))
     spread = jnp.concatenate(spread, axis=1)
     result = dot(spread, b_ref[...].reshape(per_owner * rank_width, columns))
-    blocks = columns // width
     for c in range(blocks):
         wide[pl.ds(c, total, stride=blocks), :] = result[:, c * width : (c + 1) * width]
-    for owner in range(owners):
-        back_ref[owner] = wide[owner * body : (owner + 1) * body, :].astype(jnp.bfloat16)
+    half = owners // 2
+    leaving = []
+    for start, end in ((0, half), (half, owners)):
+        for owner in range(start, end):
+            ready[owner] = wide[owner * body : (owner + 1) * body, :].astype(jnp.bfloat16)
+        few = pl.ds(start, end - start)
+        leaving.append(pltpu.make_async_copy(ready.at[few], back_ref.at[few], left.at[len(leaving)]))
+        leaving[-1].start()
+    for copy in leaving:
+        copy.wait()
 
 
 def update(own, others, slot, factor, b_store, owners):
@@ -247,62 +376,72 @@
     body = total * columns // width // owners
     return pl.pallas_call(
         update_kernel,
-        out_shape=jax.ShapeDtypeStruct((owners, body, width), jnp.bfloat16),
+        out_shape=pltpu.HBM((owners, body, width), jnp.bfloat16),
         in_specs=[pl.BlockSpec(memory_space=pltpu.VMEM)] * 5,
-        out_specs=pl.BlockSpec(memory_space=pltpu.VMEM),
-        scratch_shapes=[pltpu.VMEM((owners * body, width), jnp.float32)],
+        out_specs=pl.BlockSpec(memory_space=pl.ANY),
+        scratch_shapes=[
+            pltpu.VMEM((owners * body, width), jnp.float32),
+            pltpu.VMEM((owners, body, width), jnp.bfloat16),
+            pltpu.SemaphoreType.DMA((2,)),
+        ],
         compiler_params=pltpu.CompilerParams(vmem_limit_bytes=SMALL_VMEM),
         cost_estimate=pl.CostEstimate(
             flops=2 * total * b_store.size, bytes_accessed=2 * b_store.size, transcendentals=0
         ),
         name="update",
-    )(own, others, slot, factor, b_store)
-
-
-def finish_kernel(seat, core, back_ref, base_ref, other_ref, out_ref, wide):
+    )(own, others, slot, near(factor), near(b_store))
+
+
+def finish_kernel(parts, seat, back_ref, base_ref, out_ref, wide, ready, left):
     requests, steps, columns = out_ref.shape
     owners, body, width = back_ref.shape
     rows = body // QCAP
     blocks = columns // width
-    total = requests * steps
-    for request in range(requests):
-        owner = seat[request] // QCAP
-        turn = seat[request] % QCAP
-        wide[request * rows : (request + 1) * rows, :] = back_ref[
-            owner, pl.ds(pl.multiple_of(turn * rows, rows), rows), :
-        ].astype(jnp.float32)
-    for c in range(blocks):
-        here = slice(c * width, (c + 1) * width)
-        mixed = base_ref[:, here]
-        for k in range(other_ref.shape[0]):
-            mixed = mixed + other_ref[k, :, here].astype(jnp.float32)
-        mixed = mixed + wide[pl.ds(c, total, stride=blocks), :]
-        out_ref[:, :, here] = mixed.reshape(requests, steps, width).astype(out_ref.dtype)
-
-
-def finish(seat, core, back, partial_out, others, requests, steps, columns):
+    few = requests // parts
+    total = few * steps
+    leaving = []
+    for part in range(parts):
+        for request in range(part * few, (part + 1) * few):
+            owner, turn = seat[request] // QCAP, seat[request] % QCAP
+            wide[request * rows : (request + 1) * rows, :] = back_ref[
+                owner, pl.ds(pl.multiple_of(turn * rows, rows), rows), :
+            ].astype(jnp.float32)
+        mine = pl.ds(part * few, few)
+        for c in range(blocks):
+            here = slice(c * width, (c + 1) * width)
+            mixed = base_ref[part * total : (part + 1) * total, here]
+            mixed = mixed + wide[pl.ds(part * few * rows + c, total, stride=blocks), :]
+            ready[mine, :, here] = mixed.reshape(few, steps, width).astype(ready.dtype)
+        leaving.append(pltpu.make_async_copy(ready.at[mine], out_ref.at[mine], left.at[part]))
+        leaving[-1].start()
+    for copy in leaving:
+        copy.wait()
+
+
+def finish(seat, back, base, requests, steps):
     owners, body, width = back.shape
-    total = requests * steps
+    total, columns = base.shape
+    parts = FINISH if requests % FINISH == 0 else 1
     return pl.pallas_call(
-        finish_kernel,
-        grid_spec=pltpu.PrefetchScalarGridSpec(
-            num_scalar_prefetch=2,
-            grid=(1,),
-            in_specs=[
-                pl.BlockSpec(back.shape, lambda i, seat, core: (0, 0, 0)),
-                pl.BlockSpec((total, columns), lambda i, seat, core: (0, core[0])),
-                pl.BlockSpec(others.shape, lambda i, seat, core: (0, 0, 0)),
-            ],
-            out_specs=pl.BlockSpec((requests, steps, columns), lambda i, seat, core: (0, 0, 0)),
-            scratch_shapes=[pltpu.VMEM((requests * body // QCAP, width), jnp.float32)],
-        ),
+        functools.partial(finish_kernel, parts),
+        in_specs=[
+            pl.BlockSpec(memory_space=pltpu.SMEM),
+            pl.BlockSpec(memory_space=pltpu.VMEM),
+            pl.BlockSpec(memory_space=pltpu.VMEM),
+        ],
+        out_specs=pl.BlockSpec(memory_space=pl.ANY),
+        scratch_shapes=[
+            pltpu.VMEM((requests * body // QCAP, width), jnp.float32),
+            pltpu.VMEM((requests, steps, columns), jnp.bfloat16),
+            pltpu.SemaphoreType.DMA((parts,)),
+        ],
         out_shape=jax.ShapeDtypeStruct((requests, steps, columns), jnp.bfloat16),
         compiler_params=pltpu.CompilerParams(vmem_limit_bytes=SMALL_VMEM),
         cost_estimate=pl.CostEstimate(
-            flops=3 * total * columns, bytes_accessed=12 * total * columns, transcendentals=0
+            flops=2 * total * columns, bytes_accessed=8 * total * columns, transcendentals=0
         ),
         name="finish",
-    )(seat, core, back, partial_out, others)
+    )(seat, back, base)
 
 
 def local(queries, kv_cache, new_kv, lengths, adapter_ids, place, ranks, w_out, a_store, b_store):
@@ -320,30 +459,24 @@
     )
     got = lax.all_to_all(sent, "store", split_axis=0, concat_axis=0, tiled=True)
 
-    partial_out = jnp.dot(
-        attended.reshape(request_count * step_count, feature_half),
-        w_out,
-        preferred_element_type=jnp.float32,
+    blocks = [((core + step) % cores).reshape(1) for step in range(cores)]
+    a_turned = jnp.swapaxes(a_store, 1, 2)
+    here = (lax.axis_index("store") * per_owner).reshape(1)
+    share, x, a_near, factor = other_columns(
+        attended, w_out, blocks[1], out_half, here, place, ranks, a_turned
     )
-    here = lax.axis_index("store") * per_owner + jnp.arange(per_owner, dtype=jnp.int32)
-    slot_rank = jnp.sum(jnp.where(here[:, None] == place[None, :], ranks[None, :], 0), axis=1)
-    factor = rank_factor(slot_rank, rank_width).reshape(1, per_owner * rank_width)
-
-    got, partial_out = lax.optimization_barrier((got, partial_out))
-    own, slot = low(got, jnp.swapaxes(a_store, 1, 2), seats, step_count)
+    share = lax.ppermute(share, "tensor", shifts[0])
+
+    own, slot = low(got, a_near, seats, step_count)
     others = jnp.stack([lax.ppermute(own, "tensor", shift) for shift in shifts])
     back = update(own, others, slot, factor, b_store, owners)
-    back, partial_out = lax.optimization_barrier((back, partial_out))
+    back, x, share = lax.optimization_barrier((back, x, share))
     back = lax.all_to_all(back, "store", split_axis=0, concat_axis=0, tiled=True)
-
-    shares = []
-    for step, shift in enumerate(shifts, 1):
-        target = (core + step) % cores
-        share = lax.dynamic_slice_in_dim(partial_out, target * out_half, out_half, 1)
-        shares.append(lax.ppermute(share, "tensor", shift))
-    return finish(
-        seat, core.reshape(1), back, partial_out, jnp.stack(shares), request_count, step_count, out_half
-    )
+    for step in range(2, cores):
+        more = own_columns(x, w_out, blocks[step], out_half, jnp.zeros_like(share))
+        share = share + lax.ppermute(more, "tensor", shifts[step - 1])
+    base = own_columns(x, w_out, blocks[0], out_half, share)
+    return finish(seat, back, base, request_count, step_count)
 
 
 def solution(mesh):

time: 52.6 us -> 46.7 us (0.89)
  blocking collectives: 16 us -> 0 us
  waiting for transfers between devices: 3.49 us -> 14.4 us
  Pallas kernels: 11.6 us -> 20.8 us
  matrix products: 8.55 us -> 0 us
  local copies, waits for them, and re-layouts: 4.5 us -> 0.01 us
  starting transfers between devices: 7.59 us -> 11.1 us
    all_to_all x1 -> x0, blocking collectives: 16 us -> none  [local(): lax.all_to_all(back, 'store', split_axis=0, concat_axis=0, tiled=True)]
    pallas_call x2 -> x4, Pallas kernels: 2.43 us -> 14.1 us  [the longest x1 6.65 us: other_columns(): pl.pallas_call(other_columns_kernel, grid_spec=pltpu.PrefetchScalarGridSp...]
    dot_general x1 -> x0, matrix products: 8.55 us -> none  [local(): jnp.dot(attended.reshape(request_count * step_count, feature_half), w_out...]
    all_to_all x0 -> x1, waiting for transfers between devices: none -> 7.55 us  [local(): lax.all_to_all(back, 'store', split_axis=0, concat_axis=0, tiled=True)]
    all_to_all x0 -> x1, starting transfers between devices: none -> 3.65 us  [local(): lax.all_to_all(back, 'store', split_axis=0, concat_axis=0, tiled=True)]
    all_to_all x1, waiting for transfers between devices: 2.42 us -> 5.65 us  [local(): got = lax.all_to_all(sent, 'store', split_axis=0, concat_axis=0, tiled=True)]
    unnamed x10 -> x2, local copies, waits for them, and re-layouts: 3.19 us -> 0.01 us
    pallas_call x1, Pallas kernels: 8.32 us -> 5.73 us  [attend(): pl.pallas_call(functools.partial(attend_kernel, steps, heads, per_owner),...]
  transfers between devices with their start and end apart: 3 -> 4, of which waited for: 2 -> 3; matrix products, arithmetic and copies ran while one was open for 19% -> 0% of each run, Pallas kernels for 0% -> 29%
where the time goes in v4:
time: 46.7 us; the launch traced here: 46.3 us
  Pallas kernels  20.8 us (45%)
  waiting for transfers between devices  14.4 us (31%)
  starting transfers between devices  11.1 us (24%)
    all_to_all x1, waiting for transfers between devices, local(): lax.all_to_all(back, 'store', split_axis=0, concat_axis=0, tiled=True)  7.55 us
    all_to_all x1, starting transfers between devices, local(): got = lax.all_to_all(sent, 'store', split_axis=0, concat_axis=0, tiled=True)  7.3 us
    pallas_call x1, Pallas kernels, other_columns(): pl.pallas_call(other_columns_kernel, grid_spec=pltpu.PrefetchScalarGridSp...  6.65 us
    pallas_call x1, Pallas kernels, attend(): pl.pallas_call(functools.partial(attend_kernel, steps, heads, per_owner),...  5.73 us
    all_to_all x1, waiting for transfers between devices, local(): got = lax.all_to_all(sent, 'store', split_axis=0, concat_axis=0, tiled=True)  5.65 us
    pallas_call x1, Pallas kernels, own_columns(): pl.pallas_call(own_columns_kernel, grid_spec=pltpu.PrefetchScalarGridSpec...  4.47 us
    all_to_all x1, starting transfers between devices, local(): lax.all_to_all(back, 'store', split_axis=0, concat_axis=0, tiled=True)  3.65 us
    pallas_call x1, Pallas kernels, finish(): pl.pallas_call(functools.partial(finish_kernel, parts), in_specs=[pl.Bloc...  1.68 us
  transfers between devices with their start and end apart: 4, of which 3 were waited for; matrix products, arithmetic and copies ran while one was open for 0% of the time, Pallas kernels for 29%

profile of v4, /device:TPU:0, one launch (start us, length us, event | category | flops | bytes accessed | tf_op | source)
XLA Modules:
  0.0 46.3 jit_solution(7350486380753436650)
XLA Ops:
  0.0 5.7 %attend.1 = (bf16[24,64,128]{2,1,0:T(8,128)(2,1)S(1)}, bf16[8,208,128]{2,1,0:T(8,128)(2,1)}, s32[24]{0:T(128)S(1)}) custom-call(s32[24]{0:T(128)} %lengths.1, s32[24]{0:T(128)} %adapter_ids.1, s32[64]{0:T(128)} %place.3, bf16[24,64,128]{2,1,0:T(8,128)(2,1)} %bitcast.9, bf16[2,24,2,256,128]{4,3,2,1,0:T(8,128)(2,1)} %kv_ref.1, bf16[2,24,8,128]{3,2,1,0:T(8,128)(2,1)} %bitcast.10), custom_call_target="tpu_custom_call" | custom-call | flops 402653184 | bytes 7077888 | tf_op jit(solution)/shard_map/attend/pallas_call | solution.py:129
  5.7 7.3 %all-to-all-start = ((bf16[8,208,128]{2,1,0:T(8,128)(2,1)}), bf16[8,208,128]{2,1,0:T(8,128)(2,1)S(1)}, u32[]{:S(2)}, u32[]{:S(2)}) async-start(bf16[8,208,128]{2,1,0:T(8,128)(2,1)} %get-tuple-element.18), calls=%async_computation | async-start | bytes 851968 | tf_op jit(solution)/shard_map/all_to_all | solution.py:460
  13.0 6.6 %other_columns.1 = (f32[96,2048]{1,0:T(8,128)}, bf16[96,2048]{1,0:T(8,128)(2,1)}, bf16[8,64,2048]{2,1,0:T(8,128)(2,1)S(1)}, f32[4,128]{1,0:T(4,128)S(1)}) custom-call(s32[1]{0:T(128)} %bitcast.2.block, s32[1]{0:T(128)} %bitcast.3.here, s32[64]{0:T(128)} %place.3, s32[64]{0:T(128)} %ranks.1, bf16[24,64,128]{2,1,0:T(8,128)(2,1)S(1)} %get-tuple-element.19.attended_ref, ...), custom_call_target="tpu_custom_call" | custom-call | flops 805306368 | bytes 12582912 | tf_op jit(solution)/shard_map/other_columns/pallas_call | solution.py:220
  19.7 0.1 collective-permute-start.1
  19.8 5.6 %all-to-all-done.got_ref = bf16[8,208,128]{2,1,0:T(8,128)(2,1)S(1)} async-done(((bf16[8,208,128]{2,1,0:T(8,128)(2,1)}), bf16[8,208,128]{2,1,0:T(8,128)(2,1)S(1)}, u32[]{:S(2)}, u32[]{:S(2)}) %all-to-all-start) | async-done | bytes 426016 | tf_op jit(solution)/shard_map/all_to_all | solution.py:460
  25.4 0.0 copy-start
  25.4 0.9 %low.1 = (f32[96,128]{1,0:T(8,128)S(1)}, f32[96,128]{1,0:T(8,128)S(1)}) custom-call(bf16[8,208,128]{2,1,0:T(8,128)(2,1)S(1)} %all-to-all-done.got_ref, bf16[8,64,2048]{2,1,0:T(8,128)(2,1)S(1)} %get-tuple-element.20.a_ref), custom_call_target="tpu_custom_call" | custom-call | flops 201326592 | bytes 2097152 | tf_op jit(solution)/shard_map/low/pallas_call | solution.py:323
  26.3 0.1 collective-permute-start
  26.4 1.2 %collective-permute-done = f32[96,128]{1,0:T(8,128)S(1)} collective-permute-done((f32[96,128]{1,0:T(8,128)S(1)}, f32[96,128]{1,0:T(8,128)S(1)}, u32[]{:S(2)}, u32[]{:S(2)}) %collective-permute-start) | collective-permute-done | bytes 49184 | tf_op jit(solution)/shard_map/ppermute | solution.py:471
  27.6 0.0 copy-done
  27.6 1.3 %update.1 = bf16[8,192,128]{2,1,0:T(8,128)(2,1)} custom-call(f32[96,128]{1,0:T(8,128)S(1)} %get-tuple-element.21.own_ref, f32[1,96,128]{2,1,0:T(8,128)S(1)} %bitcast.7, f32[96,128]{1,0:T(8,128)S(1)} %get-tuple-element.22.slot_ref, f32[4,128]{1,0:T(4,128)S(1)} %get-tuple-element.23.factor_ref, bf16[8,64,2048]{2,1,0:T(8,128)(2,1)S(1)} %copy-done), custom_call_target="tpu_custom_call" | custom-call | flops 201326592 | bytes 2097152 | tf_op jit(solution)/shard_map/update/pallas_call | solution.py:377
  28.9 0.0 collective-permute-done.1.share_ref
  29.0 3.6 %all-to-all-start.1 = ((bf16[8,192,128]{2,1,0:T(8,128)(2,1)}), bf16[8,192,128]{2,1,0:T(8,128)(2,1)S(1)}, u32[]{:S(2)}, u32[]{:S(2)}) async-start(bf16[8,192,128]{2,1,0:T(8,128)(2,1)} %update.1), calls=%async_computation.1 | async-start | bytes 786432 | tf_op jit(solution)/shard_map/all_to_all | solution.py:474
  32.6 4.5 %own_columns.1.base_ref = f32[96,2048]{1,0:T(8,128)S(1)} custom-call(s32[1]{0:T(128)} %bitcast.6.block, bf16[96,2048]{1,0:T(8,128)(2,1)} %get-tuple-element.27.x_ref, bf16[2048,4096]{1,0:T(8,128)(2,1)} %w_ref.3, f32[96,2048]{1,0:T(8,128)S(1)} %collective-permute-done.1.share_ref), custom_call_target="tpu_custom_call" | custom-call | flops 805306368 | bytes 8388608 | tf_op jit(solution)/shard_map/own_columns/pallas_call | solution.py:267
  37.1 7.5 %all-to-all-done.1.back_ref = bf16[8,192,128]{2,1,0:T(8,128)(2,1)S(1)} async-done(((bf16[8,192,128]{2,1,0:T(8,128)(2,1)}), bf16[8,192,128]{2,1,0:T(8,128)(2,1)S(1)}, u32[]{:S(2)}, u32[]{:S(2)}) %all-to-all-start.1) | async-done | bytes 393248 | tf_op jit(solution)/shard_map/all_to_all | solution.py:474
  44.6 1.7 %finish.1 = bf16[24,4,2048]{2,1,0:T(4,128)(2,1)} custom-call(s32[24]{0:T(128)S(1)} %get-tuple-element.17.seat, bf16[8,192,128]{2,1,0:T(8,128)(2,1)S(1)} %all-to-all-done.1.back_ref, f32[96,2048]{1,0:T(8,128)S(1)} %own_columns.1.base_ref), custom_call_target="tpu_custom_call" | custom-call | flops 393216 | bytes 1572864 | tf_op jit(solution)/shard_map/finish/pallas_call | solution.py:425
Async XLA Ops:
  5.7 19.7 %all-to-all-start = ((bf16[8,208,128]{2,1,0:T(8,128)(2,1)}), bf16[8,208,128]{2,1,0:T(8,128)(2,1)S(1)}, u32[]{:S(2)}, u32[]{:S(2)}) async-start(bf16[8,208,128]{2,1,0:T(8,128)(2,1)} %get-tuple-element.18), calls=%async_computation | async-start | bytes 851968 | tf_op jit(solution)/shard_map/all_to_all | solution.py:460
  19.7 9.3 %collective-permute-start.1 = (f32[96,2048]{1,0:T(8,128)}, f32[96,2048]{1,0:T(8,128)S(1)}, u32[]{:S(2)}, u32[]{:S(2)}) collective-permute-start(f32[96,2048]{1,0:T(8,128)} %get-tuple-element.25), channel_id=1, source_target_pairs={{0,1},{1,0},{2,3},{3,2},{4,5},{5,4},{6,7},{7,6},{8,9},{9,8},{10,11... | collective-permute-start | bytes 2359304 | tf_op jit(solution)/shard_map/ppermute | solution.py:468
  25.4 2.2 %copy-start = (bf16[8,64,2048]{2,1,0:T(8,128)(2,1)S(1)}, bf16[8,64,2048]{2,1,0:T(8,128)(2,1)}, u32[]{:S(2)}) copy-start(bf16[8,64,2048]{2,1,0:T(8,128)(2,1)} %b_ref.1) | copy-start | bytes 6291460
  26.3 1.3 %collective-permute-start = (f32[96,128]{1,0:T(8,128)S(1)}, f32[96,128]{1,0:T(8,128)S(1)}, u32[]{:S(2)}, u32[]{:S(2)}) collective-permute-start(f32[96,128]{1,0:T(8,128)S(1)} %get-tuple-element.21.own_ref), channel_id=1, source_target_pairs={{0,1},{1,0},{2,3},{3,2},{4,5},{5,4},{6,7},{7,6},{8,9},{9,8},{10,11... | collective-permute-start | bytes 147464 | tf_op jit(solution)/shard_map/ppermute | solution.py:471
  29.0 15.7 %all-to-all-start.1 = ((bf16[8,192,128]{2,1,0:T(8,128)(2,1)}), bf16[8,192,128]{2,1,0:T(8,128)(2,1)S(1)}, u32[]{:S(2)}, u32[]{:S(2)}) async-start(bf16[8,192,128]{2,1,0:T(8,128)(2,1)} %update.1), calls=%async_computation.1 | async-start | bytes 786432 | tf_op jit(solution)/shard_map/all_to_all | solution.py:474

commit v5 on v4

--- a/solution.py
+++ b/solution.py
@@ -14,7 +14,6 @@
 ATTEND_VMEM = 24 * 1024 * 1024
 TILE = 1024
 BASE_VMEM = 32 * 1024 * 1024
-BATCH = 12
 FINISH = 2
 SMALL_VMEM = 16 * 1024 * 1024
 
@@ -36,28 +35,36 @@
 
 
 def attend_kernel(
-    steps, heads, per_owner,
+    sizes, heads, per_owner,
     lengths, adapter_ids, place,
-    q_ref, kv_ref, new_ref,
+    q_far, kv_far, new_far,
     attended_ref, sent_ref, seat_ref,
-    taken, slots,
+    q_ref, kv_ref, new_ref, taken, slots, arrived,
 ):
     owners = taken.shape[0]
-    seats = owners * QCAP
-    requests = seat_ref.shape[0]
-    batch, rows, width = q_ref.shape
+    requests, rows, width = attended_ref.shape
     slots_in_cache = kv_ref.shape[3]
     group = heads // 2
-    step = pl.program_id(0)
-
-    @pl.when(step == 0)
-    def _():
-        for owner in range(owners):
-            taken[owner] = 0
-        for seat in range(seats):
-            slots[seat] = 0
-        if seats > requests:
-            sent_ref[...] = jnp.zeros_like(sent_ref)
+    coming = [
+        pltpu.make_async_copy(q_far, q_ref, arrived.at[0]),
+        pltpu.make_async_copy(new_far, new_ref, arrived.at[1]),
+    ]
+    end = 0
+    for size in sizes:
+        few = pl.ds(end, size)
+        end = end + size
+        coming.append(
+            pltpu.make_async_copy(kv_far.at[:, few], kv_ref.at[:, few], arrived.at[len(coming)])
+        )
+    for copy in coming:
+        copy.start()
+
+    for owner in range(owners):
+        taken[owner] = 0
+    for seat in range(owners * QCAP):
+        slots[seat] = 0
+    if owners * QCAP > requests:
+        sent_ref[...] = jnp.zeros_like(sent_ref)
 
     row = lax.broadcasted_iota(jnp.int32, (rows, width), 0)
     first = (row // group) % 2 == 0
@@ -68,82 +75,87 @@
     column = lax.broadcasted_iota(jnp.int32, (rows, slots_in_cache), 1)
     scale = 1.0 / math.sqrt(width)
 
-    cached, fresh = [], []
-    for j in range(batch):
-        q = q_ref[j]
-        q_wide = q.astype(jnp.float32)
-        both = jnp.concatenate(
-            [jnp.where(first, q_wide, 0.0), jnp.where(first, 0.0, q_wide)], axis=1
-        ).astype(jnp.bfloat16)
-        keys = jnp.concatenate([kv_ref[0, j, 0], kv_ref[0, j, 1]], axis=1)
-        scores = dot(both, keys, (1, 1)) * scale
-        cached.append(jnp.where(column < lengths[step * batch + j], scores, -jnp.inf))
-        scores = dot(q, new_ref[0, j], (1, 1)) * scale
-        fresh.append(jnp.where(new_seen, scores, -jnp.inf))
-    tops = [
-        jnp.maximum(jnp.max(a, axis=1, keepdims=True), jnp.max(b, axis=1, keepdims=True))
-        for a, b in zip(cached, fresh)
-    ]
-    cached = [jnp.exp(a - top) for a, top in zip(cached, tops)]
-    fresh = [jnp.exp(b - top) for b, top in zip(fresh, tops)]
-    sums = [
-        1.0 / (jnp.sum(a, axis=1, keepdims=True) + jnp.sum(b, axis=1, keepdims=True))
-        for a, b in zip(cached, fresh)
-    ]
-    cached = [(a * inv).astype(jnp.bfloat16) for a, inv in zip(cached, sums)]
-    fresh = [(b * inv).astype(jnp.bfloat16) for b, inv in zip(fresh, sums)]
-    for j in range(batch):
-        values = jnp.concatenate([kv_ref[1, j, 0], kv_ref[1, j, 1]], axis=1)
-        both = dot(cached[j], values)
-        result = jnp.where(first, both[:, :width], both[:, width:]) + dot(fresh[j], new_ref[1, j])
-        result = result.astype(jnp.bfloat16)
-        request = step * batch + j
-        location = place[adapter_ids[request]]
-        owner = location // per_owner
-        turn = taken[owner]
-        taken[owner] = turn + 1
-        slots[owner * QCAP + turn] = location % per_owner
-        seat_ref[request] = owner * QCAP + turn
-        attended_ref[request] = result
-        sent_ref[owner, pl.ds(pl.multiple_of(turn * rows, rows), rows), :] = result
-
-    @pl.when(step == steps - 1)
-    def _():
-        note_row = lax.broadcasted_iota(jnp.int32, (NOTE, width), 0)
-        per_seat = rows // heads
-        for owner in range(owners):
-            note = jnp.zeros((NOTE, width), jnp.int32)
-            for turn in range(QCAP):
-                note = jnp.where(note_row // per_seat == turn, slots[owner * QCAP + turn], note)
-            sent_ref[owner, QCAP * rows :, :] = note.astype(jnp.float32).astype(jnp.bfloat16)
+    coming[0].wait()
+    coming[1].wait()
+    end = 0
+    for size, copy in zip(sizes, coming[2:]):
+        start, end = end, end + size
+        copy.wait()
+        cached, fresh = [], []
+        for r in range(start, end):
+            q = q_ref[r]
+            q_wide = q.astype(jnp.float32)
+            both = jnp.concatenate(
+                [jnp.where(first, q_wide, 0.0), jnp.where(first, 0.0, q_wide)], axis=1
+            ).astype(jnp.bfloat16)
+            keys = jnp.concatenate([kv_ref[0, r, 0], kv_ref[0, r, 1]], axis=1)
+            scores = dot(both, keys, (1, 1)) * scale
+            cached.append(jnp.where(column < lengths[r], scores, -jnp.inf))
+            scores = dot(q, new_ref[0, r], (1, 1)) * scale
+            fresh.append(jnp.where(new_seen, scores, -jnp.inf))
+        tops = [
+            jnp.maximum(jnp.max(a, axis=1, keepdims=True), jnp.max(b, axis=1, keepdims=True))
+            for a, b in zip(cached, fresh)
+        ]
+        cached = [jnp.exp(a - top) for a, top in zip(cached, tops)]
+        fresh = [jnp.exp(b - top) for b, top in zip(fresh, tops)]
+        sums = [
+            1.0 / (jnp.sum(a, axis=1, keepdims=True) + jnp.sum(b, axis=1, keepdims=True))
+            for a, b in zip(cached, fresh)
+        ]
+        cached = [(a * inv).astype(jnp.bfloat16) for a, inv in zip(cached, sums)]
+        fresh = [(b * inv).astype(jnp.bfloat16) for b, inv in zip(fresh, sums)]
+        for a, b, r in zip(cached, fresh, range(start, end)):
+            values = jnp.concatenate([kv_ref[1, r, 0], kv_ref[1, r, 1]], axis=1)
+            both = dot(a, values)
+            result = jnp.where(first, both[:, :width], both[:, width:]) + dot(b, new_ref[1, r])
+            result = result.astype(jnp.bfloat16)
+            location = place[adapter_ids[r]]
+            owner = location // per_owner
+            turn = taken[owner]
+            taken[owner] = turn + 1
+            slots[owner * QCAP + turn] = location % per_owner
+            seat_ref[r] = owner * QCAP + turn
+            attended_ref[r] = result
+            sent_ref[owner, pl.ds(pl.multiple_of(turn * rows, rows), rows), :] = result
+
+    note_row = lax.broadcasted_iota(jnp.int32, (NOTE, width), 0)
+    per_seat = rows // heads
+    for owner in range(owners):
+        note = jnp.zeros((NOTE, width), jnp.int32)
+        for turn in range(QCAP):
+            note = jnp.where(note_row // per_seat == turn, slots[owner * QCAP + turn], note)
+        sent_ref[owner, QCAP * rows :, :] = note.astype(jnp.float32).astype(jnp.bfloat16)
 
 
 def attend(queries, kv_cache, new_kv, lengths, adapter_ids, place, owners, per_owner):
     requests, step_count, heads, width = queries.shape
-    cache_slots = kv_cache.shape[3]
     rows = step_count * heads
     new_rows = new_kv.shape[2] * new_kv.shape[3]
-    batch = BATCH if requests % BATCH == 0 else 1
-    steps = requests // batch
     body = QCAP * rows + NOTE
+    sizes = [requests // 6, requests // 3]
+    sizes = [size for size in [*sizes, requests - sum(sizes)] if size]
+    queries = queries.reshape(requests, rows, width)
+    new_kv = new_kv.reshape(2, requests, new_rows, width)
+    anywhere = pl.BlockSpec(memory_space=pl.ANY)
     return pl.pallas_call(
-        functools.partial(attend_kernel, steps, heads, per_owner),
+        functools.partial(attend_kernel, sizes, heads, per_owner),
         grid_spec=pltpu.PrefetchScalarGridSpec(
             num_scalar_prefetch=3,
-            grid=(steps,),
-            in_specs=[
-                pl.BlockSpec((batch, rows, width), lambda i, *_: (i, 0, 0)),
-                pl.BlockSpec((2, batch, 2, cache_slots, width), lambda i, *_: (0, i, 0, 0, 0)),
-                pl.BlockSpec((2, batch, new_rows, width), lambda i, *_: (0, i, 0, 0)),
-            ],
+            grid=(1,),
+            in_specs=[anywhere, anywhere, anywhere],
             out_specs=[
                 pl.BlockSpec(memory_space=pltpu.VMEM),
                 pl.BlockSpec((owners, body, width), lambda i, *_: (0, 0, 0)),
                 pl.BlockSpec(memory_space=pltpu.SMEM),
             ],
             scratch_shapes=[
+                pltpu.VMEM(queries.shape, queries.dtype),
+                pltpu.VMEM(kv_cache.shape, kv_cache.dtype),
+                pltpu.VMEM(new_kv.shape, new_kv.dtype),
                 pltpu.SMEM((owners,), jnp.int32),
                 pltpu.SMEM((owners * QCAP,), jnp.int32),
+                pltpu.SemaphoreType.DMA((2 + len(sizes),)),
             ],
         ),
         out_shape=[
@@ -155,19 +167,12 @@
             dimension_semantics=("arbitrary",), vmem_limit_bytes=ATTEND_VMEM
         ),
         cost_estimate=pl.CostEstimate(
-            flops=4 * requests * rows * cache_slots * width * 2,
+            flops=4 * requests * rows * kv_cache.shape[3] * width * 2,
             bytes_accessed=kv_cache.size * 2 + 4 * queries.size,
-            transcendentals=requests * rows * cache_slots,
+            transcendentals=requests * rows * kv_cache.shape[3],
         ),
         name="attend",
-    )(
-        far(lengths),
-        far(adapter_ids),
-        far(place),
-        far(queries.reshape(requests, rows, width)),
-        far(kv_cache),
-        far(new_kv.reshape(2, requests, new_rows, width)),
-    )
+    )(far(lengths), far(adapter_ids), far(place), far(queries), far(kv_cache), far(new_kv))
 
 
 def other_columns_kernel(

time: 46.7 us -> 46.6 us (level)
  no operation moved by 1% of the time
where the time goes in v5:
time: 46.6 us; the launch traced here: 46.2 us
  Pallas kernels  20.7 us (44%)
  waiting for transfers between devices  14.4 us (31%)
  starting transfers between devices  11.1 us (24%)
    all_to_all x1, waiting for transfers between devices, local(): lax.all_to_all(back, 'store', split_axis=0, concat_axis=0, tiled=True)  7.55 us
    all_to_all x1, starting transfers between devices, local(): got = lax.all_to_all(sent, 'store', split_axis=0, concat_axis=0, tiled=True)  7.29 us
    pallas_call x1, Pallas kernels, other_columns(): pl.pallas_call(other_columns_kernel, grid_spec=pltpu.PrefetchScalarGridSp...  6.65 us
    all_to_all x1, waiting for transfers between devices, local(): got = lax.all_to_all(sent, 'store', split_axis=0, concat_axis=0, tiled=True)  5.65 us
    pallas_call x1, Pallas kernels, attend(): pl.pallas_call(functools.partial(attend_kernel, sizes, heads, per_owner),...  5.63 us
    pallas_call x1, Pallas kernels, own_columns(): pl.pallas_call(own_columns_kernel, grid_spec=pltpu.PrefetchScalarGridSpec...  4.47 us
    all_to_all x1, starting transfers between devices, local(): lax.all_to_all(back, 'store', split_axis=0, concat_axis=0, tiled=True)  3.65 us
    pallas_call x1, Pallas kernels, finish(): pl.pallas_call(functools.partial(finish_kernel, parts), in_specs=[pl.Bloc...  1.68 us
  transfers between devices with their start and end apart: 4, of which 3 were waited for; matrix products, arithmetic and copies ran while one was open for 0% of the time, Pallas kernels for 29%

profile of v5, /device:TPU:0, one launch (start us, length us, event | category | flops | bytes accessed | tf_op | source)
XLA Modules:
  0.0 46.2 jit_solution(18205735775398386708)
XLA Ops:
  0.0 5.6 %attend.1 = (bf16[24,64,128]{2,1,0:T(8,128)(2,1)S(1)}, bf16[8,208,128]{2,1,0:T(8,128)(2,1)}, s32[24]{0:T(128)S(1)}) custom-call(s32[24]{0:T(128)} %lengths.1, s32[24]{0:T(128)} %adapter_ids.1, s32[64]{0:T(128)} %place.3, bf16[24,64,128]{2,1,0:T(8,128)(2,1)} %bitcast.9, bf16[2,24,2,256,128]{4,3,2,1,0:T(8,128)(2,1)} %kv_far.1, bf16[2,24,8,128]{3,2,1,0:T(8,128)(2,1)} %bitcast.10), custom_call_target="tpu_custom_call" | custom-call | flops 402653184 | bytes 7077888 | tf_op jit(solution)/shard_map/attend/pallas_call | solution.py:141
  5.6 7.3 %all-to-all-start = ((bf16[8,208,128]{2,1,0:T(8,128)(2,1)}), bf16[8,208,128]{2,1,0:T(8,128)(2,1)S(1)}, u32[]{:S(2)}, u32[]{:S(2)}) async-start(bf16[8,208,128]{2,1,0:T(8,128)(2,1)} %get-tuple-element.18), calls=%async_computation | async-start | bytes 851968 | tf_op jit(solution)/shard_map/all_to_all | solution.py:465
  12.9 6.6 %other_columns.1 = (f32[96,2048]{1,0:T(8,128)}, bf16[96,2048]{1,0:T(8,128)(2,1)}, bf16[8,64,2048]{2,1,0:T(8,128)(2,1)S(1)}, f32[4,128]{1,0:T(4,128)S(1)}) custom-call(s32[1]{0:T(128)} %bitcast.2.block, s32[1]{0:T(128)} %bitcast.3.here, s32[64]{0:T(128)} %place.3, s32[64]{0:T(128)} %ranks.1, bf16[24,64,128]{2,1,0:T(8,128)(2,1)S(1)} %get-tuple-element.19.attended_ref, ...), custom_call_target="tpu_custom_call" | custom-call | flops 805306368 | bytes 12582912 | tf_op jit(solution)/shard_map/other_columns/pallas_call | solution.py:225
  19.6 0.1 collective-permute-start.1
  19.7 5.6 %all-to-all-done.got_ref = bf16[8,208,128]{2,1,0:T(8,128)(2,1)S(1)} async-done(((bf16[8,208,128]{2,1,0:T(8,128)(2,1)}), bf16[8,208,128]{2,1,0:T(8,128)(2,1)S(1)}, u32[]{:S(2)}, u32[]{:S(2)}) %all-to-all-start) | async-done | bytes 426016 | tf_op jit(solution)/shard_map/all_to_all | solution.py:465
  25.3 0.0 copy-start
  25.3 0.9 %low.1 = (f32[96,128]{1,0:T(8,128)S(1)}, f32[96,128]{1,0:T(8,128)S(1)}) custom-call(bf16[8,208,128]{2,1,0:T(8,128)(2,1)S(1)} %all-to-all-done.got_ref, bf16[8,64,2048]{2,1,0:T(8,128)(2,1)S(1)} %get-tuple-element.20.a_ref), custom_call_target="tpu_custom_call" | custom-call | flops 201326592 | bytes 2097152 | tf_op jit(solution)/shard_map/low/pallas_call | solution.py:328
  26.2 0.1 collective-permute-start
  26.3 1.2 %collective-permute-done = f32[96,128]{1,0:T(8,128)S(1)} collective-permute-done((f32[96,128]{1,0:T(8,128)S(1)}, f32[96,128]{1,0:T(8,128)S(1)}, u32[]{:S(2)}, u32[]{:S(2)}) %collective-permute-start) | collective-permute-done | bytes 49184 | tf_op jit(solution)/shard_map/ppermute | solution.py:476
  27.5 0.0 copy-done
  27.5 1.3 %update.1 = bf16[8,192,128]{2,1,0:T(8,128)(2,1)} custom-call(f32[96,128]{1,0:T(8,128)S(1)} %get-tuple-element.21.own_ref, f32[1,96,128]{2,1,0:T(8,128)S(1)} %bitcast.7, f32[96,128]{1,0:T(8,128)S(1)} %get-tuple-element.22.slot_ref, f32[4,128]{1,0:T(4,128)S(1)} %get-tuple-element.23.factor_ref, bf16[8,64,2048]{2,1,0:T(8,128)(2,1)S(1)} %copy-done), custom_call_target="tpu_custom_call" | custom-call | flops 201326592 | bytes 2097152 | tf_op jit(solution)/shard_map/update/pallas_call | solution.py:382
  28.9 0.0 collective-permute-done.1.share_ref
  28.9 3.6 %all-to-all-start.1 = ((bf16[8,192,128]{2,1,0:T(8,128)(2,1)}), bf16[8,192,128]{2,1,0:T(8,128)(2,1)S(1)}, u32[]{:S(2)}, u32[]{:S(2)}) async-start(bf16[8,192,128]{2,1,0:T(8,128)(2,1)} %update.1), calls=%async_computation.1 | async-start | bytes 786432 | tf_op jit(solution)/shard_map/all_to_all | solution.py:479
  32.5 4.5 %own_columns.1.base_ref = f32[96,2048]{1,0:T(8,128)S(1)} custom-call(s32[1]{0:T(128)} %bitcast.6.block, bf16[96,2048]{1,0:T(8,128)(2,1)} %get-tuple-element.27.x_ref, bf16[2048,4096]{1,0:T(8,128)(2,1)} %w_ref.3, f32[96,2048]{1,0:T(8,128)S(1)} %collective-permute-done.1.share_ref), custom_call_target="tpu_custom_call" | custom-call | flops 805306368 | bytes 8388608 | tf_op jit(solution)/shard_map/own_columns/pallas_call | solution.py:272
  37.0 7.6 %all-to-all-done.1.back_ref = bf16[8,192,128]{2,1,0:T(8,128)(2,1)S(1)} async-done(((bf16[8,192,128]{2,1,0:T(8,128)(2,1)}), bf16[8,192,128]{2,1,0:T(8,128)(2,1)S(1)}, u32[]{:S(2)}, u32[]{:S(2)}) %all-to-all-start.1) | async-done | bytes 393248 | tf_op jit(solution)/shard_map/all_to_all | solution.py:479
  44.5 1.7 %finish.1 = bf16[24,4,2048]{2,1,0:T(4,128)(2,1)} custom-call(s32[24]{0:T(128)S(1)} %get-tuple-element.17.seat, bf16[8,192,128]{2,1,0:T(8,128)(2,1)S(1)} %all-to-all-done.1.back_ref, f32[96,2048]{1,0:T(8,128)S(1)} %own_columns.1.base_ref), custom_call_target="tpu_custom_call" | custom-call | flops 393216 | bytes 1572864 | tf_op jit(solution)/shard_map/finish/pallas_call | solution.py:430
Async XLA Ops:
  5.6 19.7 %all-to-all-start = ((bf16[8,208,128]{2,1,0:T(8,128)(2,1)}), bf16[8,208,128]{2,1,0:T(8,128)(2,1)S(1)}, u32[]{:S(2)}, u32[]{:S(2)}) async-start(bf16[8,208,128]{2,1,0:T(8,128)(2,1)} %get-tuple-element.18), calls=%async_computation | async-start | bytes 851968 | tf_op jit(solution)/shard_map/all_to_all | solution.py:465
  19.6 9.3 %collective-permute-start.1 = (f32[96,2048]{1,0:T(8,128)}, f32[96,2048]{1,0:T(8,128)S(1)}, u32[]{:S(2)}, u32[]{:S(2)}) collective-permute-start(f32[96,2048]{1,0:T(8,128)} %get-tuple-element.25), channel_id=1, source_target_pairs={{0,1},{1,0},{2,3},{3,2},{4,5},{5,4},{6,7},{7,6},{8,9},{9,8},{10,11... | collective-permute-start | bytes 2359304 | tf_op jit(solution)/shard_map/ppermute | solution.py:473
  25.3 2.2 %copy-start = (bf16[8,64,2048]{2,1,0:T(8,128)(2,1)S(1)}, bf16[8,64,2048]{2,1,0:T(8,128)(2,1)}, u32[]{:S(2)}) copy-start(bf16[8,64,2048]{2,1,0:T(8,128)(2,1)} %b_ref.1) | copy-start | bytes 6291460
  26.2 1.3 %collective-permute-start = (f32[96,128]{1,0:T(8,128)S(1)}, f32[96,128]{1,0:T(8,128)S(1)}, u32[]{:S(2)}, u32[]{:S(2)}) collective-permute-start(f32[96,128]{1,0:T(8,128)S(1)} %get-tuple-element.21.own_ref), channel_id=1, source_target_pairs={{0,1},{1,0},{2,3},{3,2},{4,5},{5,4},{6,7},{7,6},{8,9},{9,8},{10,11... | collective-permute-start | bytes 147464 | tf_op jit(solution)/shard_map/ppermute | solution.py:476
  28.9 15.7 %all-to-all-start.1 = ((bf16[8,192,128]{2,1,0:T(8,128)(2,1)}), bf16[8,192,128]{2,1,0:T(8,128)(2,1)S(1)}, u32[]{:S(2)}, u32[]{:S(2)}) async-start(bf16[8,192,128]{2,1,0:T(8,128)(2,1)} %update.1), calls=%async_computation.1 | async-start | bytes 786432 | tf_op jit(solution)/shard_map/all_to_all | solution.py:479

commit v6 on v5

--- a/solution.py
+++ b/solution.py
@@ -47,7 +47,7 @@
     group = heads // 2
     coming = [
         pltpu.make_async_copy(q_far, q_ref, arrived.at[0]),
-        pltpu.make_async_copy(new_far, new_ref, arrived.at[1]),
+        pltpu.make_async_copy(new_far, new_ref.at[:, pl.ds(0, requests)], arrived.at[1]),
     ]
     end = 0
     for size in sizes:
@@ -152,7 +152,7 @@
             scratch_shapes=[
                 pltpu.VMEM(queries.shape, queries.dtype),
                 pltpu.VMEM(kv_cache.shape, kv_cache.dtype),
-                pltpu.VMEM(new_kv.shape, new_kv.dtype),
+                pltpu.VMEM((2, requests + 1, new_rows, width), new_kv.dtype),
                 pltpu.SMEM((owners,), jnp.int32),
                 pltpu.SMEM((owners * QCAP,), jnp.int32),
                 pltpu.SemaphoreType.DMA((2 + len(sizes),)),
@@ -292,7 +292,7 @@
     )(block, far(x), far(w_out), share)
 
 
-def low_kernel(seats, steps, got_ref, a_ref, low_ref, slot_ref, wide):
+def low_kernel(seats, steps, got_ref, a_ref, low_ref, slot_ref, wide, spare):
     owners, rows, width = got_ref.shape
     body = rows - NOTE
     per_owner, rank_width, features = a_ref.shape
@@ -305,11 +305,12 @@
     )
     per_group = total // owners
     for owner in range(owners):
-        slot_ref[owner * per_group : (owner + 1) * per_group, :] = got_ref[owner, body:, :].astype(
+        spare[owner * per_group : (owner + 1) * per_group, :] = got_ref[owner, body:, :].astype(
             jnp.float32
         )[:per_group]
     every = dot(x, a_ref[...].reshape(per_owner * rank_width, features), (1, 1))
-    slot = slot_ref[...].astype(jnp.int32)
+    slot_ref[...] = spare[:total]
+    slot = spare[:total].astype(jnp.int32)
     lane = lax.broadcasted_iota(jnp.int32, (total, width), 1)
     per_block = width // rank_width
     kept = jnp.zeros((total, width), jnp.float32)
@@ -333,7 +334,10 @@
         ],
         in_specs=[pl.BlockSpec(memory_space=pltpu.VMEM)] * 2,
         out_specs=[pl.BlockSpec(memory_space=pltpu.VMEM)] * 2,
-        scratch_shapes=[pltpu.VMEM((owners * (rows - NOTE), width), jnp.float32)],
+        scratch_shapes=[
+            pltpu.VMEM((owners * (rows - NOTE), width), jnp.float32),
+            pltpu.VMEM((total + NOTE, width), jnp.float32),
+        ],
         compiler_params=pltpu.CompilerParams(vmem_limit_bytes=SMALL_VMEM),
         cost_estimate=pl.CostEstimate(
             flops=2 * total * a_turned.size, bytes_accessed=2 * a_turned.size, transcendentals=0
@@ -437,7 +441,7 @@
         out_specs=pl.BlockSpec(memory_space=pl.ANY),
         scratch_shapes=[
             pltpu.VMEM((requests * body // QCAP, width), jnp.float32),
-            pltpu.VMEM((requests, steps, columns), jnp.bfloat16),
+            pltpu.VMEM((requests + 2, steps, columns), jnp.bfloat16),
             pltpu.SemaphoreType.DMA((parts,)),
         ],
         out_shape=jax.ShapeDtypeStruct((requests, steps, columns), jnp.bfloat16),

time: 46.6 us -> 46.6 us (level)
  no operation moved by 1% of the time
where the time goes in v6:
time: 46.6 us; the launch traced here: 46.2 us
  Pallas kernels  20.7 us (44%)
  waiting for transfers between devices  14.4 us (31%)
  starting transfers between devices  11.1 us (24%)
    all_to_all x1, waiting for transfers between devices, local(): lax.all_to_all(back, 'store', split_axis=0, concat_axis=0, tiled=True)  7.55 us
    all_to_all x1, starting transfers between devices, local(): got = lax.all_to_all(sent, 'store', split_axis=0, concat_axis=0, tiled=True)  7.3 us
    pallas_call x1, Pallas kernels, other_columns(): pl.pallas_call(other_columns_kernel, grid_spec=pltpu.PrefetchScalarGridSp...  6.65 us
    all_to_all x1, waiting for transfers between devices, local(): got = lax.all_to_all(sent, 'store', split_axis=0, concat_axis=0, tiled=True)  5.65 us
    pallas_call x1, Pallas kernels, attend(): pl.pallas_call(functools.partial(attend_kernel, sizes, heads, per_owner),...  5.63 us
    pallas_call x1, Pallas kernels, own_columns(): pl.pallas_call(own_columns_kernel, grid_spec=pltpu.PrefetchScalarGridSpec...  4.47 us
    all_to_all x1, starting transfers between devices, local(): lax.all_to_all(back, 'store', split_axis=0, concat_axis=0, tiled=True)  3.65 us
    pallas_call x1, Pallas kernels, finish(): pl.pallas_call(functools.partial(finish_kernel, parts), in_specs=[pl.Bloc...  1.68 us
  transfers between devices with their start and end apart: 4, of which 3 were waited for; matrix products, arithmetic and copies ran while one was open for 0% of the time, Pallas kernels for 29%

profile of v6, /device:TPU:0, one launch (start us, length us, event | category | flops | bytes accessed | tf_op | source)
XLA Modules:
  0.0 46.2 jit_solution(12204571642403954380)
XLA Ops:
  0.0 5.6 %attend.1 = (bf16[24,64,128]{2,1,0:T(8,128)(2,1)S(1)}, bf16[8,208,128]{2,1,0:T(8,128)(2,1)}, s32[24]{0:T(128)S(1)}) custom-call(s32[24]{0:T(128)} %lengths.1, s32[24]{0:T(128)} %adapter_ids.1, s32[64]{0:T(128)} %place.3, bf16[24,64,128]{2,1,0:T(8,128)(2,1)} %bitcast.9, bf16[2,24,2,256,128]{4,3,2,1,0:T(8,128)(2,1)} %kv_far.1, bf16[2,24,8,128]{3,2,1,0:T(8,128)(2,1)} %bitcast.10), custom_call_target="tpu_custom_call" | custom-call | flops 402653184 | bytes 7077888 | tf_op jit(solution)/shard_map/attend/pallas_call | solution.py:141
  5.6 7.3 %all-to-all-start = ((bf16[8,208,128]{2,1,0:T(8,128)(2,1)}), bf16[8,208,128]{2,1,0:T(8,128)(2,1)S(1)}, u32[]{:S(2)}, u32[]{:S(2)}) async-start(bf16[8,208,128]{2,1,0:T(8,128)(2,1)} %get-tuple-element.18), calls=%async_computation | async-start | bytes 851968 | tf_op jit(solution)/shard_map/all_to_all | solution.py:469
  12.9 6.6 %other_columns.1 = (f32[96,2048]{1,0:T(8,128)}, bf16[96,2048]{1,0:T(8,128)(2,1)}, bf16[8,64,2048]{2,1,0:T(8,128)(2,1)S(1)}, f32[4,128]{1,0:T(4,128)S(1)}) custom-call(s32[1]{0:T(128)} %bitcast.2.block, s32[1]{0:T(128)} %bitcast.3.here, s32[64]{0:T(128)} %place.3, s32[64]{0:T(128)} %ranks.1, bf16[24,64,128]{2,1,0:T(8,128)(2,1)S(1)} %get-tuple-element.19.attended_ref, ...), custom_call_target="tpu_custom_call" | custom-call | flops 805306368 | bytes 12582912 | tf_op jit(solution)/shard_map/other_columns/pallas_call | solution.py:225
  19.6 0.1 collective-permute-start.1
  19.7 5.6 %all-to-all-done.got_ref = bf16[8,208,128]{2,1,0:T(8,128)(2,1)S(1)} async-done(((bf16[8,208,128]{2,1,0:T(8,128)(2,1)}), bf16[8,208,128]{2,1,0:T(8,128)(2,1)S(1)}, u32[]{:S(2)}, u32[]{:S(2)}) %all-to-all-start) | async-done | bytes 426016 | tf_op jit(solution)/shard_map/all_to_all | solution.py:469
  25.3 0.0 copy-start
  25.3 0.9 %low.1 = (f32[96,128]{1,0:T(8,128)S(1)}, f32[96,128]{1,0:T(8,128)S(1)}) custom-call(bf16[8,208,128]{2,1,0:T(8,128)(2,1)S(1)} %all-to-all-done.got_ref, bf16[8,64,2048]{2,1,0:T(8,128)(2,1)S(1)} %get-tuple-element.20.a_ref), custom_call_target="tpu_custom_call" | custom-call | flops 201326592 | bytes 2097152 | tf_op jit(solution)/shard_map/low/pallas_call | solution.py:329
  26.2 0.1 collective-permute-start
  26.3 1.2 %collective-permute-done = f32[96,128]{1,0:T(8,128)S(1)} collective-permute-done((f32[96,128]{1,0:T(8,128)S(1)}, f32[96,128]{1,0:T(8,128)S(1)}, u32[]{:S(2)}, u32[]{:S(2)}) %collective-permute-start) | collective-permute-done | bytes 49184 | tf_op jit(solution)/shard_map/ppermute | solution.py:480
  27.5 0.0 copy-done
  27.5 1.3 %update.1 = bf16[8,192,128]{2,1,0:T(8,128)(2,1)} custom-call(f32[96,128]{1,0:T(8,128)S(1)} %get-tuple-element.21.own_ref, f32[1,96,128]{2,1,0:T(8,128)S(1)} %bitcast.7, f32[96,128]{1,0:T(8,128)S(1)} %get-tuple-element.22.slot_ref, f32[4,128]{1,0:T(4,128)S(1)} %get-tuple-element.23.factor_ref, bf16[8,64,2048]{2,1,0:T(8,128)(2,1)S(1)} %copy-done), custom_call_target="tpu_custom_call" | custom-call | flops 201326592 | bytes 2097152 | tf_op jit(solution)/shard_map/update/pallas_call | solution.py:386
  28.9 0.0 collective-permute-done.1.share_ref
  28.9 3.6 %all-to-all-start.1 = ((bf16[8,192,128]{2,1,0:T(8,128)(2,1)}), bf16[8,192,128]{2,1,0:T(8,128)(2,1)S(1)}, u32[]{:S(2)}, u32[]{:S(2)}) async-start(bf16[8,192,128]{2,1,0:T(8,128)(2,1)} %update.1), calls=%async_computation.1 | async-start | bytes 786432 | tf_op jit(solution)/shard_map/all_to_all | solution.py:483
  32.5 4.5 %own_columns.1.base_ref = f32[96,2048]{1,0:T(8,128)S(1)} custom-call(s32[1]{0:T(128)} %bitcast.6.block, bf16[96,2048]{1,0:T(8,128)(2,1)} %get-tuple-element.27.x_ref, bf16[2048,4096]{1,0:T(8,128)(2,1)} %w_ref.3, f32[96,2048]{1,0:T(8,128)S(1)} %collective-permute-done.1.share_ref), custom_call_target="tpu_custom_call" | custom-call | flops 805306368 | bytes 8388608 | tf_op jit(solution)/shard_map/own_columns/pallas_call | solution.py:272
  37.0 7.6 %all-to-all-done.1.back_ref = bf16[8,192,128]{2,1,0:T(8,128)(2,1)S(1)} async-done(((bf16[8,192,128]{2,1,0:T(8,128)(2,1)}), bf16[8,192,128]{2,1,0:T(8,128)(2,1)S(1)}, u32[]{:S(2)}, u32[]{:S(2)}) %all-to-all-start.1) | async-done | bytes 393248 | tf_op jit(solution)/shard_map/all_to_all | solution.py:483
  44.5 1.7 %finish.1 = bf16[24,4,2048]{2,1,0:T(4,128)(2,1)} custom-call(s32[24]{0:T(128)S(1)} %get-tuple-element.17.seat, bf16[8,192,128]{2,1,0:T(8,128)(2,1)S(1)} %all-to-all-done.1.back_ref, f32[96,2048]{1,0:T(8,128)S(1)} %own_columns.1.base_ref), custom_call_target="tpu_custom_call" | custom-call | flops 393216 | bytes 1572864 | tf_op jit(solution)/shard_map/finish/pallas_call | solution.py:434
Async XLA Ops:
  5.6 19.7 %all-to-all-start = ((bf16[8,208,128]{2,1,0:T(8,128)(2,1)}), bf16[8,208,128]{2,1,0:T(8,128)(2,1)S(1)}, u32[]{:S(2)}, u32[]{:S(2)}) async-start(bf16[8,208,128]{2,1,0:T(8,128)(2,1)} %get-tuple-element.18), calls=%async_computation | async-start | bytes 851968 | tf_op jit(solution)/shard_map/all_to_all | solution.py:469
  19.6 9.3 %collective-permute-start.1 = (f32[96,2048]{1,0:T(8,128)}, f32[96,2048]{1,0:T(8,128)S(1)}, u32[]{:S(2)}, u32[]{:S(2)}) collective-permute-start(f32[96,2048]{1,0:T(8,128)} %get-tuple-element.25), channel_id=1, source_target_pairs={{0,1},{1,0},{2,3},{3,2},{4,5},{5,4},{6,7},{7,6},{8,9},{9,8},{10,11... | collective-permute-start | bytes 2359304 | tf_op jit(solution)/shard_map/ppermute | solution.py:477
  25.3 2.2 %copy-start = (bf16[8,64,2048]{2,1,0:T(8,128)(2,1)S(1)}, bf16[8,64,2048]{2,1,0:T(8,128)(2,1)}, u32[]{:S(2)}) copy-start(bf16[8,64,2048]{2,1,0:T(8,128)(2,1)} %b_ref.1) | copy-start | bytes 6291460
  26.2 1.3 %collective-permute-start = (f32[96,128]{1,0:T(8,128)S(1)}, f32[96,128]{1,0:T(8,128)S(1)}, u32[]{:S(2)}, u32[]{:S(2)}) collective-permute-start(f32[96,128]{1,0:T(8,128)S(1)} %get-tuple-element.21.own_ref), channel_id=1, source_target_pairs={{0,1},{1,0},{2,3},{3,2},{4,5},{5,4},{6,7},{7,6},{8,9},{9,8},{10,11... | collective-permute-start | bytes 147464 | tf_op jit(solution)/shard_map/ppermute | solution.py:480
  28.9 15.7 %all-to-all-start.1 = ((bf16[8,192,128]{2,1,0:T(8,128)(2,1)}), bf16[8,192,128]{2,1,0:T(8,128)(2,1)S(1)}, u32[]{:S(2)}, u32[]{:S(2)}) async-start(bf16[8,192,128]{2,1,0:T(8,128)(2,1)} %update.1), calls=%async_computation.1 | async-start | bytes 786432 | tf_op jit(solution)/shard_map/all_to_all | solution.py:483

commit v7 on v6

--- a/solution.py
+++ b/solution.py
@@ -103,13 +103,13 @@
             1.0 / (jnp.sum(a, axis=1, keepdims=True) + jnp.sum(b, axis=1, keepdims=True))
             for a, b in zip(cached, fresh)
         ]
-        cached = [(a * inv).astype(jnp.bfloat16) for a, inv in zip(cached, sums)]
-        fresh = [(b * inv).astype(jnp.bfloat16) for b, inv in zip(fresh, sums)]
-        for a, b, r in zip(cached, fresh, range(start, end)):
+        cached = [a.astype(jnp.bfloat16) for a in cached]
+        fresh = [b.astype(jnp.bfloat16) for b in fresh]
+        for a, b, inv, r in zip(cached, fresh, sums, range(start, end)):
             values = jnp.concatenate([kv_ref[1, r, 0], kv_ref[1, r, 1]], axis=1)
             both = dot(a, values)
             result = jnp.where(first, both[:, :width], both[:, width:]) + dot(b, new_ref[1, r])
-            result = result.astype(jnp.bfloat16)
+            result = (result * inv).astype(jnp.bfloat16)
             location = place[adapter_ids[r]]
             owner = location // per_owner
             turn = taken[owner]

time: 46.6 us -> 46.6 us (level)
  no operation moved by 1% of the time
where the time goes in v7:
time: 46.6 us; the launch traced here: 46.2 us
  Pallas kernels  20.7 us (44%)
  waiting for transfers between devices  14.4 us (31%)
  starting transfers between devices  11.1 us (24%)
    all_to_all x1, waiting for transfers between devices, local(): lax.all_to_all(back, 'store', split_axis=0, concat_axis=0, tiled=True)  7.54 us
    all_to_all x1, starting transfers between devices, local(): got = lax.all_to_all(sent, 'store', split_axis=0, concat_axis=0, tiled=True)  7.29 us
    pallas_call x1, Pallas kernels, other_columns(): pl.pallas_call(other_columns_kernel, grid_spec=pltpu.PrefetchScalarGridSp...  6.65 us
    all_to_all x1, waiting for transfers between devices, local(): got = lax.all_to_all(sent, 'store', split_axis=0, concat_axis=0, tiled=True)  5.65 us
    pallas_call x1, Pallas kernels, attend(): pl.pallas_call(functools.partial(attend_kernel, sizes, heads, per_owner),...  5.62 us
    pallas_call x1, Pallas kernels, own_columns(): pl.pallas_call(own_columns_kernel, grid_spec=pltpu.PrefetchScalarGridSpec...  4.47 us
    all_to_all x1, starting transfers between devices, local(): lax.all_to_all(back, 'store', split_axis=0, concat_axis=0, tiled=True)  3.65 us
    pallas_call x1, Pallas kernels, finish(): pl.pallas_call(functools.partial(finish_kernel, parts), in_specs=[pl.Bloc...  1.68 us
  transfers between devices with their start and end apart: 4, of which 3 were waited for; matrix products, arithmetic and copies ran while one was open for 0% of the time, Pallas kernels for 29%

profile of v7, /device:TPU:0, one launch (start us, length us, event | category | flops | bytes accessed | tf_op | source)
XLA Modules:
  0.0 46.2 jit_solution(8750623856972779595)
XLA Ops:
  0.0 5.6 %attend.1 = (bf16[24,64,128]{2,1,0:T(8,128)(2,1)S(1)}, bf16[8,208,128]{2,1,0:T(8,128)(2,1)}, s32[24]{0:T(128)S(1)}) custom-call(s32[24]{0:T(128)} %lengths.1, s32[24]{0:T(128)} %adapter_ids.1, s32[64]{0:T(128)} %place.3, bf16[24,64,128]{2,1,0:T(8,128)(2,1)} %bitcast.9, bf16[2,24,2,256,128]{4,3,2,1,0:T(8,128)(2,1)} %kv_far.1, bf16[2,24,8,128]{3,2,1,0:T(8,128)(2,1)} %bitcast.10), custom_call_target="tpu_custom_call" | custom-call | flops 402653184 | bytes 7077888 | tf_op jit(solution)/shard_map/attend/pallas_call | solution.py:141
  5.6 7.3 %all-to-all-start = ((bf16[8,208,128]{2,1,0:T(8,128)(2,1)}), bf16[8,208,128]{2,1,0:T(8,128)(2,1)S(1)}, u32[]{:S(2)}, u32[]{:S(2)}) async-start(bf16[8,208,128]{2,1,0:T(8,128)(2,1)} %get-tuple-element.18), calls=%async_computation | async-start | bytes 851968 | tf_op jit(solution)/shard_map/all_to_all | solution.py:469
  12.9 6.6 %other_columns.1 = (f32[96,2048]{1,0:T(8,128)}, bf16[96,2048]{1,0:T(8,128)(2,1)}, bf16[8,64,2048]{2,1,0:T(8,128)(2,1)S(1)}, f32[4,128]{1,0:T(4,128)S(1)}) custom-call(s32[1]{0:T(128)} %bitcast.2.block, s32[1]{0:T(128)} %bitcast.3.here, s32[64]{0:T(128)} %place.3, s32[64]{0:T(128)} %ranks.1, bf16[24,64,128]{2,1,0:T(8,128)(2,1)S(1)} %get-tuple-element.19.attended_ref, ...), custom_call_target="tpu_custom_call" | custom-call | flops 805306368 | bytes 12582912 | tf_op jit(solution)/shard_map/other_columns/pallas_call | solution.py:225
  19.6 0.1 collective-permute-start.1
  19.7 5.6 %all-to-all-done.got_ref = bf16[8,208,128]{2,1,0:T(8,128)(2,1)S(1)} async-done(((bf16[8,208,128]{2,1,0:T(8,128)(2,1)}), bf16[8,208,128]{2,1,0:T(8,128)(2,1)S(1)}, u32[]{:S(2)}, u32[]{:S(2)}) %all-to-all-start) | async-done | bytes 426016 | tf_op jit(solution)/shard_map/all_to_all | solution.py:469
  25.3 0.0 copy-start
  25.3 0.9 %low.1 = (f32[96,128]{1,0:T(8,128)S(1)}, f32[96,128]{1,0:T(8,128)S(1)}) custom-call(bf16[8,208,128]{2,1,0:T(8,128)(2,1)S(1)} %all-to-all-done.got_ref, bf16[8,64,2048]{2,1,0:T(8,128)(2,1)S(1)} %get-tuple-element.20.a_ref), custom_call_target="tpu_custom_call" | custom-call | flops 201326592 | bytes 2097152 | tf_op jit(solution)/shard_map/low/pallas_call | solution.py:329
  26.2 0.1 collective-permute-start
  26.3 1.2 %collective-permute-done = f32[96,128]{1,0:T(8,128)S(1)} collective-permute-done((f32[96,128]{1,0:T(8,128)S(1)}, f32[96,128]{1,0:T(8,128)S(1)}, u32[]{:S(2)}, u32[]{:S(2)}) %collective-permute-start) | collective-permute-done | bytes 49184 | tf_op jit(solution)/shard_map/ppermute | solution.py:480
  27.5 0.0 copy-done
  27.5 1.3 %update.1 = bf16[8,192,128]{2,1,0:T(8,128)(2,1)} custom-call(f32[96,128]{1,0:T(8,128)S(1)} %get-tuple-element.21.own_ref, f32[1,96,128]{2,1,0:T(8,128)S(1)} %bitcast.7, f32[96,128]{1,0:T(8,128)S(1)} %get-tuple-element.22.slot_ref, f32[4,128]{1,0:T(4,128)S(1)} %get-tuple-element.23.factor_ref, bf16[8,64,2048]{2,1,0:T(8,128)(2,1)S(1)} %copy-done), custom_call_target="tpu_custom_call" | custom-call | flops 201326592 | bytes 2097152 | tf_op jit(solution)/shard_map/update/pallas_call | solution.py:386
  28.8 0.0 collective-permute-done.1.share_ref
  28.9 3.7 %all-to-all-start.1 = ((bf16[8,192,128]{2,1,0:T(8,128)(2,1)}), bf16[8,192,128]{2,1,0:T(8,128)(2,1)S(1)}, u32[]{:S(2)}, u32[]{:S(2)}) async-start(bf16[8,192,128]{2,1,0:T(8,128)(2,1)} %update.1), calls=%async_computation.1 | async-start | bytes 786432 | tf_op jit(solution)/shard_map/all_to_all | solution.py:483
  32.5 4.5 %own_columns.1.base_ref = f32[96,2048]{1,0:T(8,128)S(1)} custom-call(s32[1]{0:T(128)} %bitcast.6.block, bf16[96,2048]{1,0:T(8,128)(2,1)} %get-tuple-element.27.x_ref, bf16[2048,4096]{1,0:T(8,128)(2,1)} %w_ref.3, f32[96,2048]{1,0:T(8,128)S(1)} %collective-permute-done.1.share_ref), custom_call_target="tpu_custom_call" | custom-call | flops 805306368 | bytes 8388608 | tf_op jit(solution)/shard_map/own_columns/pallas_call | solution.py:272
  37.0 7.5 %all-to-all-done.1.back_ref = bf16[8,192,128]{2,1,0:T(8,128)(2,1)S(1)} async-done(((bf16[8,192,128]{2,1,0:T(8,128)(2,1)}), bf16[8,192,128]{2,1,0:T(8,128)(2,1)S(1)}, u32[]{:S(2)}, u32[]{:S(2)}) %all-to-all-start.1) | async-done | bytes 393248 | tf_op jit(solution)/shard_map/all_to_all | solution.py:483
  44.5 1.7 %finish.1 = bf16[24,4,2048]{2,1,0:T(4,128)(2,1)} custom-call(s32[24]{0:T(128)S(1)} %get-tuple-element.17.seat, bf16[8,192,128]{2,1,0:T(8,128)(2,1)S(1)} %all-to-all-done.1.back_ref, f32[96,2048]{1,0:T(8,128)S(1)} %own_columns.1.base_ref), custom_call_target="tpu_custom_call" | custom-call | flops 393216 | bytes 1572864 | tf_op jit(solution)/shard_map/finish/pallas_call | solution.py:434
Async XLA Ops:
  5.6 19.7 %all-to-all-start = ((bf16[8,208,128]{2,1,0:T(8,128)(2,1)}), bf16[8,208,128]{2,1,0:T(8,128)(2,1)S(1)}, u32[]{:S(2)}, u32[]{:S(2)}) async-start(bf16[8,208,128]{2,1,0:T(8,128)(2,1)} %get-tuple-element.18), calls=%async_computation | async-start | bytes 851968 | tf_op jit(solution)/shard_map/all_to_all | solution.py:469
  19.6 9.3 %collective-permute-start.1 = (f32[96,2048]{1,0:T(8,128)}, f32[96,2048]{1,0:T(8,128)S(1)}, u32[]{:S(2)}, u32[]{:S(2)}) collective-permute-start(f32[96,2048]{1,0:T(8,128)} %get-tuple-element.25), channel_id=1, source_target_pairs={{0,1},{1,0},{2,3},{3,2},{4,5},{5,4},{6,7},{7,6},{8,9},{9,8},{10,11... | collective-permute-start | bytes 2359304 | tf_op jit(solution)/shard_map/ppermute | solution.py:477
  25.3 2.2 %copy-start = (bf16[8,64,2048]{2,1,0:T(8,128)(2,1)S(1)}, bf16[8,64,2048]{2,1,0:T(8,128)(2,1)}, u32[]{:S(2)}) copy-start(bf16[8,64,2048]{2,1,0:T(8,128)(2,1)} %b_ref.1) | copy-start | bytes 6291460
  26.2 1.3 %collective-permute-start = (f32[96,128]{1,0:T(8,128)S(1)}, f32[96,128]{1,0:T(8,128)S(1)}, u32[]{:S(2)}, u32[]{:S(2)}) collective-permute-start(f32[96,128]{1,0:T(8,128)S(1)} %get-tuple-element.21.own_ref), channel_id=1, source_target_pairs={{0,1},{1,0},{2,3},{3,2},{4,5},{5,4},{6,7},{7,6},{8,9},{9,8},{10,11... | collective-permute-start | bytes 147464 | tf_op jit(solution)/shard_map/ppermute | solution.py:480
  28.9 15.7 %all-to-all-start.1 = ((bf16[8,192,128]{2,1,0:T(8,128)(2,1)}), bf16[8,192,128]{2,1,0:T(8,128)(2,1)S(1)}, u32[]{:S(2)}, u32[]{:S(2)}) async-start(bf16[8,192,128]{2,1,0:T(8,128)(2,1)} %update.1), calls=%async_computation.1 | async-start | bytes 786432 | tf_op jit(solution)/shard_map/all_to_all | solution.py:483
